TPU v7x, 256 devices: a whole 4x4x8 slice. The times are simulated.
256 devices in a mesh: dp: 32 (over z, x), tensor: 8 (over y, core).
Axes of the slice: x: 4, y: 4, z: 8, core: 2. Of those that a mesh axis runs over, the one named last changes fastest.
Arguments:
- prompt_states: bfloat16 [128, 256, 5120], P('dp', None, 'tensor'), may hold values from -18 to 18
- prompt_lengths: int32 [128], replicated, may hold values from 1 to 256, 16384 in all
- decode_states: bfloat16 [2048, 4, 5120], P('dp', None, 'tensor'), may hold values from -18 to 18
- sample_owner: int32 [2048, 1], P('dp'), may hold values from 0 to 31; in each aligned block of 64 rows (0 to 63, 64 to 127, ...) at most 4 rows name the same one
- sample_local: int32 [2048], P('dp'), may hold values from 0 to 3
- norm_gain: float32 [5120], P('tensor'), may hold values from 0.5 to 2
- kv_weight: bfloat16 [5120, 8, 256], P(None, 'tensor'), may hold values from -1 to 1
- q_weight: bfloat16 [5120, 8, 384], P(None, 'tensor'), may hold values from -1 to 1
- output_weight: bfloat16 [8, 384, 5120], P('tensor'), may hold values from -0.3125 to 0.3125
Outputs:
- layer_out: bfloat16 [2048, 4, 5120], P('dp', None, 'tensor')
Inputs may be any that keep to these rules, and one draw needn't show every extreme that they name: `prompt_lengths`: the longest prompt has exactly 256 live positions. `sample_owner`: among the 64 samples of one dp index at most 4 name the same owner; in some dp index one owner is named exactly 4 times.
All inputs are finite; a program needn't handle non-finite values.
Results may differ from a plain program's by a relative error of at most 0.03.
Values may be sent and summed in bfloat16 or wider, within the bound.
A program may use at most 128 MiB of HBM per device.

v0:
```python
import jax
import jax.numpy as jnp
from jax import lax
from jax.sharding import PartitionSpec as P

MODEL_WIDTH = 5120


EPSILON = 1e-06
HUGE_NEGATIVE = -1e30


def softmax_part(scores, usable, value_rows, pattern):
    scores = jnp.where(usable, scores, HUGE_NEGATIVE)
    highest = jnp.max(scores, axis=-1)
    weights = jnp.where(usable, jnp.exp(scores - highest[..., None]), 0.0)
    weight_sum = jnp.sum(weights, axis=-1)
    blended = jnp.einsum(
        pattern, weights.astype(jnp.bfloat16), value_rows, preferred_element_type=jnp.float32
    )
    return (highest, weight_sum, blended)


def own_part(queries, own_rows):
    head_size = queries.shape[-1]
    scores = jnp.einsum(
        "nthqe,nuhe->nthqu", queries, own_rows[..., :head_size], preferred_element_type=jnp.float32
    ) * head_size ** (-0.5)
    step_ids = jnp.arange(queries.shape[1], dtype=jnp.int32)
    usable = (step_ids[None, :] <= step_ids[:, None])[None, :, None, None, :]
    return softmax_part(scores, usable, own_rows[..., head_size:], "nthqu,nuhe->nthqe")


def prefix_slots(slot_queries, stored, usable, score_form, blend_form):
    head_size = slot_queries.shape[-1]
    scores = jnp.einsum(
        score_form, slot_queries, stored[..., :head_size], preferred_element_type=jnp.float32
    ) * head_size ** (-0.5)
    scores = jnp.where(usable, scores, HUGE_NEGATIVE)
    highest = jnp.max(scores, axis=(-2, -1))
    weights = jnp.where(usable, jnp.exp(scores - highest[..., None, None]), 0.0)
    weight_sum = jnp.sum(weights, axis=(-2, -1))
    blended = jnp.einsum(
        blend_form,
        weights.astype(jnp.bfloat16),
        stored[..., head_size:],
        preferred_element_type=jnp.float32,
    )
    return (highest, weight_sum, blended)


def merge_parts(former, latter):
    highest = jnp.maximum(former[0], latter[0])
    factor_one = jnp.exp(former[0] - highest)
    factor_two = jnp.exp(latter[0] - highest)
    numerator = former[2] * factor_one[..., None] + latter[2] * factor_two[..., None]
    denominator = former[1] * factor_one + latter[1] * factor_two
    return (numerator / denominator[..., None]).astype(jnp.bfloat16)


def shards(
    prompt_states,
    prompt_lengths,
    decode_states,
    sample_owner,
    sample_local,
    norm_gain,
    kv_weight,
    q_weight,
    output_weight,
):
    prompts_here, longest, _ = prompt_states.shape
    samples_here, step_count, _ = decode_states.shape
    heads_here = kv_weight.shape[1]
    head_size = kv_weight.shape[2] // 2
    per_group = q_weight.shape[2] // head_size
    prompt_wide = prompt_states.astype(jnp.float32)
    decode_wide = decode_states.astype(jnp.float32)
    prompt_square, decode_square = lax.psum(
        (jnp.sum(prompt_wide * prompt_wide, axis=-1), jnp.sum(decode_wide * decode_wide, axis=-1)),
        "tensor",
    )
    prompt_factor = lax.rsqrt(prompt_square / MODEL_WIDTH + EPSILON)
    decode_factor = lax.rsqrt(decode_square / MODEL_WIDTH + EPSILON)
    prompt_scaled = (prompt_wide * norm_gain).astype(jnp.bfloat16)
    decode_scaled = (decode_wide * norm_gain).astype(jnp.bfloat16)
    prompt_sum = jnp.einsum(
        "pld,dhc->plhc",
        lax.all_gather(prompt_scaled, "tensor", axis=2, tiled=True),
        kv_weight,
        preferred_element_type=jnp.float32,
    )
    prompt_cache = (prompt_sum * prompt_factor[..., None, None]).astype(jnp.bfloat16)
    shard_piece = lax.all_gather(decode_scaled, "tensor", axis=2, tiled=True)
    query_part = jnp.einsum(
        "std,dhc->sthc", shard_piece, q_weight, preferred_element_type=jnp.float32
    )
    pair_part = jnp.einsum(
        "std,dhc->sthc", shard_piece, kv_weight, preferred_element_type=jnp.float32
    )
    queries = (query_part * decode_factor[..., None, None]).astype(jnp.bfloat16)
    queries = queries.reshape(samples_here, step_count, heads_here, per_group, head_size)
    own_cache = (pair_part * decode_factor[..., None, None]).astype(jnp.bfloat16)
    owner_of = sample_owner[:, 0]
    owner_total = lax.axis_size("dp")
    slot_depth = max(2, 2 * samples_here // owner_total)
    matches = (owner_of[:, None] == jnp.arange(owner_total, dtype=jnp.int32)[None, :]).astype(
        jnp.int32
    )
    earlier = jnp.cumsum(matches, axis=0) - matches
    target = owner_of * slot_depth + jnp.sum(earlier * matches, axis=1)
    slot_total = owner_total * slot_depth
    outgoing = jnp.zeros((slot_total,) + queries.shape[1:], jnp.bfloat16).at[target].set(queries)
    positions = jnp.arange(longest, dtype=jnp.int32)
    prompt_ids = jnp.arange(prompts_here, dtype=jnp.int32)
    every_cache = lax.all_gather(prompt_cache, "dp", axis=0, tiled=True)
    stored = every_cache.reshape((owner_total, prompts_here) + prompt_cache.shape[1:])
    slot_prompt = (
        jnp.zeros((slot_total,), jnp.int32)
        .at[target]
        .set(sample_local)
        .reshape(owner_total, slot_depth)
    )
    all_lengths = prompt_lengths.reshape(owner_total, prompts_here)
    usable = (prompt_ids[None, None, :, None] == slot_prompt[:, :, None, None]) & (
        positions[None, None, None, :] < all_lengths[:, None, :, None]
    )
    usable = usable[:, :, None, None, None, :, :]
    highest, weight_sum, blended = prefix_slots(
        outgoing.reshape((owner_total, slot_depth) + queries.shape[1:]),
        stored,
        usable,
        "octhqe,oplhe->octhqpl",
        "octhqpl,oplhe->octhqe",
    )

    def pick_slots(values):
        return jnp.take(values.reshape((slot_total,) + values.shape[2:]), target, axis=0)

    prefix = (pick_slots(highest), pick_slots(weight_sum), pick_slots(blended))
    attended = merge_parts(prefix, own_part(queries, own_cache))
    flattened = attended.reshape(samples_here, step_count, heads_here, per_group * head_size)
    partial_value = jnp.einsum(
        "sthc,hcd->sthd", flattened, output_weight, preferred_element_type=jnp.float32
    ).astype(jnp.bfloat16)
    partial_value = lax.optimization_barrier(partial_value).astype(jnp.float32)
    summed = lax.psum_scatter(
        partial_value.astype(jnp.bfloat16), "tensor", scatter_dimension=3, tiled=True
    ).astype(jnp.float32)
    return jnp.sum(summed, axis=2).astype(jnp.bfloat16)


def solution(mesh):
    placed = (
        P("dp", None, "tensor"),
        P(),
        P("dp", None, "tensor"),
        P("dp", None),
        P("dp"),
        P("tensor"),
        P(None, "tensor", None),
        P(None, "tensor", None),
        P("tensor", None, None),
    )
    return jax.shard_map(
        shards, mesh=mesh, in_specs=placed, out_specs=P("dp", None, "tensor"), check_vma=False
    )
```

profile of v0, /device:TPU:1, one launch (start us, length us, event | category | flops | bytes accessed | tf_op | source)
XLA Modules:
  0.0 340.3 jit_solution(3098989779912081917)
XLA Ops:
  6.5 2.9 fusion.11
  9.5 1.8 fusion.44
  11.4 15.2 %all-reduce = (f32[4,256]{1,0:T(4,128)S(1)}, f32[64,4]{0,1:T(4,128)S(1)}) all-reduce(f32[4,256]{1,0:T(4,128)S(1)} %get-tuple-element.12, f32[64,4]{0,1:T(4,128)S(1)} %get-tuple-element.15), channel_id=1, replica_groups=mesh['dp'=32,'tensor'=8] {'tensor'}, use_global_device_ids=true, to_apply=%region_3.0 | all-reduce | flops 1280 | bytes 10240 | tf_op jit(solution)/shard_map/psum | solution.py:79
  26.7 48.2 %all-gather.5.cloned.1.call-done = bf16[4,256,5120]{2,1,0:T(8,128)(2,1)} async-done(((bf16[4,256,640]{2,1,0:T(8,128)(2,1)}), bf16[4,256,5120]{2,1,0:T(8,128)(2,1)}) %all-gather.5.cloned.1.call-update) | async-done | bytes 10485776 | tf_op jit(solution)/shard_map/all_gather | solution.py:89
  74.9 7.7 %fusion.19 = bf16[4,256,256]{2,1,0:T(8,128)(2,1)} fusion(bf16[4,256,5120]{2,1,0:T(8,128)(2,1)} %all-gather.5.cloned.1.call-done, bf16[5120,1,256]{2,0,1:T(8,128)(2,1)S(1)} %copy-done, f32[4,256]{1,0:T(4,128)S(1)} %add_rsqrt_fusion), kind=kOutput, calls=%fused_computation.29 | convolution fusion | flops 2684878848 | bytes 13635584 | tf_op jit(solution)/shard_map/pld,dhc->plhc/dot_general | solution.py:87
  83.1 0.9 scatter_custom_fusion
  84.6 21.5 %all-gather.7.cloned.1.call-done = bf16[64,4,5120]{2,0,1:T(8,128)(2,1)} async-done(((bf16[64,4,640]{2,0,1:T(8,128)(2,1)}), bf16[64,4,5120]{2,0,1:T(8,128)(2,1)}) %all-gather.7.cloned.1.call-update) | async-done | bytes 2621456 | tf_op jit(solution)/shard_map/all_gather | solution.py:94
  106.1 4.4 %fusion.31 = bf16[64,4,384]{2,0,1:T(8,128)(2,1)S(1)} fusion(bf16[64,4,5120]{2,0,1:T(8,128)(2,1)} %all-gather.7.cloned.1.call-done, bf16[5120,1,384]{2,0,1:T(8,128)(2,1)} %param.18, f32[64,4]{0,1:T(4,128)S(1)} %add_rsqrt_fusion.1), kind=kOutput, calls=%fused_computation.39 | convolution fusion | flops 1006829568 | bytes 6751232 | tf_op jit(solution)/shard_map/std,dhc->sthc/dot_general | solution.py:95
  110.9 2.7 scatter_fusion
  113.7 2.6 fusion.40
  116.3 1.4 fusion.70
  117.7 0.5 copy.51
  119.1 129.7 %all-gather.9.cloned.1.call-done = bf16[128,256,256]{2,1,0:T(8,128)(2,1)} async-done(((bf16[4,256,256]{2,1,0:T(8,128)(2,1)}), bf16[128,256,256]{2,1,0:T(8,128)(2,1)}) %all-gather.9.cloned.1.call-update) | async-done | bytes 16777232 | tf_op jit(solution)/shard_map/all_gather | solution.py:116
  248.8 7.8 %fusion.3 = (f32[32,4,4,3]{2,3,1,0:T(4,128)S(1)}, f32[32,4,256,4,4,3]{2,4,5,3,1,0:T(4,128)}) fusion(pred[32,4,4,256]{3,1,2,0:T(4,128)(4,1)S(1)} %broadcast_and_fusion, bf16[32,4,4,3,128,1]{4,2,3,1,5,0:T(4,128)(2,1)S(1)} %bitcast.207, bf16[32,4,256,1,256]{4,2,1,0,3:T(8,128)(2,1)} %bitcast.216), kind=kOutput, calls=%fused_computation.13 | convolution fusion | flops 407370240 | bytes 15210496 | tf_op jit(solution)/shard_map/octhqe,oplhe->octhqpl/dot_general | solution.py:36
  256.6 8.4 %fusion.1 = f32[32,128,4,4,3,1]{1,3,4,2,5,0:T(4,128)S(1)} fusion(bf16[32,4,256,1,256]{4,2,1,0,3:T(8,128)(2,1)} %bitcast.217, f32[32,4,256,4,4,3]{2,4,5,3,1,0:T(4,128)} %get-tuple-element.22, f32[32,4,4,3]{2,3,1,0:T(4,128)S(1)} %get-tuple-element.21, pred[32,4,4,256]{3,1,2,0:T(4,128)(4,1)S(1)} %broadcast_and_fusion), kind=kOutput, calls=%fused_computation.8 | convolution fusion | flops 410517504 | bytes 15603712 | tf_op jit(solution)/shard_map/octhqpl,oplhe->octhqe/dot_general | solution.py:43
  265.0 6.5 %fusion.9 = f32[32,4,4,3]{2,3,1,0:T(4,128)S(1)} fusion(f32[32,4,4,3]{2,3,1,0:T(4,128)S(1)} %get-tuple-element.21, f32[32,4,256,4,4,3]{2,4,5,3,1,0:T(4,128)} %get-tuple-element.22, pred[32,4,4,256]{3,1,2,0:T(4,128)(4,1)S(1)} %broadcast_and_fusion), kind=kLoop, calls=%fused_computation.21 | loop fusion | flops 7862784 | bytes 6434816 | tf_op jit(solution)/shard_map/reduce_sum | solution.py:42
  271.5 0.9 copy.48
  272.4 0.9 copy.56
  273.3 0.7 gather_fusion.1
  273.9 0.7 gather_fusion.2
  274.8 0.5 copy.52
  275.3 0.5 copy.58
  275.8 0.5 copy.55
  276.3 0.8 gather_fusion
  277.1 1.5 fusion.30
  278.9 3.6 %fusion.2 = bf16[64,4,1,5120]{3,0,1,2:T(8,128)(2,1)S(1)} fusion(bf16[64,4,384]{2,0,1:T(8,128)(2,1)S(1)} %reshape.190, bf16[1,384,5120]{2,1,0:T(8,128)(2,1)} %param.19), kind=kOutput, calls=%fused_computation.12 | convolution fusion | flops 1007943680 | bytes 6750208 | tf_op jit(solution)/shard_map/sthc,hcd->sthd/dot_general | solution.py:143
  282.5 5.8 %copy.72 = bf16[64,4,1,5120]{0,1,2,3:T(4,128)(2,1)} copy(bf16[64,4,1,5120]{3,0,1,2:T(8,128)(2,1)S(1)} %fusion.2) | data formatting | bytes 5242880
  288.4 8.5 %reshape.264 = bf16[5120,256]{1,0:T(8,128)(2,1)} reshape(bf16[5120,1,4,64]{3,2,1,0:T(4,128)(2,1)} %bitcast.204) | data formatting | bytes 5242880
  296.9 32.2 %reduce-scatter.4.cloned.1.call-done = bf16[640,256]{1,0:T(8,128)(2,1)} async-done(((bf16[5120,256]{1,0:T(8,128)(2,1)}), bf16[640,256]{1,0:T(8,128)(2,1)}) %reduce-scatter.4.cloned.1.call-update) | async-done | bytes 327696
  329.1 1.3 reshape.265
  330.4 1.4 copy.73
  331.8 2.0 copy.60
  (40 shorter events, 3.0 us)
Async XLA Ops:
  6.5 68.4 %copy-start = (bf16[5120,1,256]{2,0,1:T(8,128)(2,1)S(1)}, bf16[5120,1,256]{2,0,1:T(8,128)(2,1)}, u32[]{:S(2)}) copy-start(bf16[5120,1,256]{2,0,1:T(8,128)(2,1)} %param.17) | copy-start | bytes 7864324
  6.5 68.4 %all-gather.5.cloned.1.call-start = ((), (), s32[]{:S(2)}) async-start(), calls=%async_computation.1 | async-start | bytes 11796480 | tf_op jit(solution)/shard_map/all_gather | solution.py:89
  9.5 96.6 %all-gather.7.cloned.1.call-start = ((), (), s32[]{:S(2)}) async-start(), calls=%async_computation.2 | async-start | bytes 2949120 | tf_op jit(solution)/shard_map/all_gather | solution.py:94
  11.4 237.4 %all-gather.9.cloned.1.call-start = ((), (), s32[]{:S(2)}) async-start(), calls=%async_computation.3 | async-start | bytes 17301504 | tf_op jit(solution)/shard_map/all_gather | solution.py:116
  26.7 56.0 %copy-start.3 = (s32[128]{0:T(128)S(1)}, s32[128]{0:T(128)}, u32[]{:S(2)}) copy-start(s32[128]{0:T(128)} %param.12) | copy-start | bytes 1540
  26.7 56.1 %copy-start.2 = (s32[64,1]{0,1:T(1,128)S(1)}, s32[64,1]{0,1:T(1,128)}, u32[]{:S(2)}) copy-start(s32[64,1]{0,1:T(1,128)} %param.14) | copy-start | bytes 772
  82.6 246.5 %reduce-scatter.4.cloned.1.call-start = ((), (), s32[]{:S(2)}) async-start(), calls=%async_computation.4 | async-start | bytes 2949120
  288.4 45.4 %copy-start.1 = (bf16[5120,1,256]{2,0,1:T(8,128)(2,1)S(1)}, bf16[5120,1,256]{2,0,1:T(8,128)(2,1)}, u32[]{:S(2)}) copy-start(bf16[5120,1,256]{2,0,1:T(8,128)(2,1)} %param.17) | copy-start | bytes 7864324
Sparse Core Ops, SparseCore 0:
  9.6 65.2 all-gather.4
  76.7 29.2 all-gather.6
  108.6 140.1 all-gather.8
  297.0 32.0 reduce-scatter.3
where the time goes:
time: 343 us; the launch traced here: 340 us
  waiting for transfers between devices  232 us (68%)
  matrix products  37.4 us (11%)
  local copies, waits for them, and re-layouts  30 us (9%)
  blocking collectives  15.2 us (4%)
  between operations  13.4 us (4%)
  other arithmetic  12.6 us (4%)
    all_gather x1, waiting for transfers between devices, shards(): every_cache = lax.all_gather(prompt_cache, 'dp', axis=0, tiled=True)  130 us
    all_gather x1, waiting for transfers between devices, shards(): lax.all_gather(prompt_scaled, 'tensor', axis=2, tiled=True)  48.2 us
    unnamed x5, waiting for transfers between devices  32.2 us
    all_gather x1, waiting for transfers between devices, shards(): shard_piece = lax.all_gather(decode_scaled, 'tensor', axis=2, tiled=True)  21.5 us
    unnamed x12, local copies, waits for them, and re-layouts  17.1 us
    psum x1, blocking collectives, shards(): lax.psum((jnp.sum(prompt_wide * prompt_wide, axis=-1), jnp.sum(decode_wid...  15.2 us
    dot_general x1, matrix products, prefix_slots(): jnp.einsum(blend_form, weights.astype(jnp.bfloat16), stored[..., head_siz...  8.38 us
    dot_general x1, matrix products, prefix_slots(): jnp.einsum(score_form, slot_queries, stored[..., :head_size], preferred_e...  7.82 us
  transfers between devices with their start and end apart: 4, of which 4 were waited for; matrix products, arithmetic and copies ran while one was open for 7% of the time, Pallas kernels for 0%

commit v1 on v0

v1 whole, which is shorter than its diff:
```python
import jax
import jax.numpy as jnp
from jax import lax
from jax.experimental import pallas as pl
from jax.experimental.pallas import tpu as pltpu
from jax.sharding import PartitionSpec as P

MESH = pl.DeviceIdType.MESH
F32 = jnp.float32
BF16 = jnp.bfloat16

MODEL_WIDTH = 5120
EPSILON = 1e-06
HUGE_NEGATIVE = -1e30

NX, NZ, NY, NC = 4, 8, 4, 2
NDP = NX * NZ
NT = NY * NC
D = 640
HEAD = 128
GROUP = 3
PROMPTS = 4
LP = 256
PR = PROMPTS * LP
HALF = PR // 2
DR = 256
DHALF = DR // 2
SLOTS = 16
WIDTH = GROUP * HEAD + 2 * HEAD
SLICE = 80

G_CORE = 0
G_UP_A, G_UP_B, G_DN_B, G_DN_A = 1, 2, 3, 4
G_UP_FA, G_DN_FB = 5, 6
G_REL = 7
SQ = 13
PS = 20
WY = 21
WZ_UP = 24
WZ_DN = 28
WX = 31
RP = 43
IDS, QX, RX = 49, 50, 51
AX = 52
WO = 53
RO = 57
N_SEM = 63


def nn(a, b):
    return lax.dot_general(a, b, (((1,), (0,)), ((), ())), preferred_element_type=F32)


def nt(a, b):
    return lax.dot_general(a, b, (((1,), (1,)), ((), ())), preferred_element_type=F32)


def iota(shape, dim):
    return lax.broadcasted_iota(jnp.int32, shape, dim)


def kernel(
    decode_hbm, prompt_hbm, gain_ref, which_ref, owner_row_ref, owner_col_ref, lengths_ref,
    kv_hbm, q_hbm, wo_hbm,
    out_ref,
    dec_raw, prm_raw, dg, ps, sg, ids, qw, kvw, wt, wob,
    rp_send, rp_recv, own_sum, kc, acc, qo, qr, ro_, rr, ax, rs_send, rs_recv,
    pid_ref, len_ref, rcol,
    ss, rs, ls,
):
    d = lax.axis_index("dp")
    t = lax.axis_index("tensor")
    z, x = d // NX, d % NX
    y, c = t // NC, t % NC
    oc = 1 - c

    def at_y(j):
        return (d, ((y + j) % NY) * NC + c)

    def at_z(j):
        return (((z + j) % NZ) * NX + x, t)

    def at_x(j):
        return (z * NX + (x + j) % NX, t)

    core = (d, y * NC + oc)
    up, dn = at_y(1), at_y(NY - 1)

    def block_of(j):
        return ((y + j) % NY) * NC + c

    def remote(src, dst, n, dev):
        return pltpu.make_async_remote_copy(
            src_ref=src, dst_ref=dst, send_sem=ss.at[n], recv_sem=rs.at[n],
            device_id=dev, device_id_type=MESH,
        )

    sent = []

    def send(src, dst, n, dev):
        copy = remote(src, dst, n, dev)
        copy.start()
        sent.append(copy)
        return copy

    l_dec = pltpu.make_async_copy(decode_hbm, dec_raw, ls.at[0])
    l_prm = pltpu.make_async_copy(prompt_hbm, prm_raw, ls.at[1])
    l_kv = pltpu.make_async_copy(kv_hbm, kvw, ls.at[2])
    l_q = pltpu.make_async_copy(q_hbm, qw, ls.at[3])
    l_wt = pltpu.make_async_copy(
        kv_hbm.at[pl.ds(pl.multiple_of(y * (2 * D), 2 * D), 2 * D)], wt.at[0], ls.at[4]
    )
    l_dec.start()
    l_prm.start()
    l_kv.start()
    l_wt.start()
    l_q.start()
    l_wo = []
    for b in range(NY):
        cols = pl.ds(pl.multiple_of((2 * b + c) * D, 128), D)
        copy = pltpu.make_async_copy(wo_hbm.at[:, cols], wob.at[0, b], ls.at[5 + b])
        copy.start()
        l_wo.append(copy)

    barrier = pltpu.get_barrier_semaphore()
    for k in range(1, NT):
        pl.semaphore_signal(barrier, inc=1, device_id=(d, (t + k) % NT), device_id_type=MESH)

    def greet(k, carry):
        pl.semaphore_signal(barrier, inc=1, device_id=((d + k) % NDP, t), device_id_type=MESH)
        return carry

    lax.fori_loop(1, NDP, greet, 0)
    pl.semaphore_wait(barrier, NT - 1 + NDP - 1)

    l_kv.wait()
    my_cols = pl.ds(pl.multiple_of((x // 2) * 128, 128), 128)
    my_row = ((x % 2) * NZ + z) * SLICE
    wy = {}
    for n, j in enumerate((2, 1, 3)):
        src_row = pl.multiple_of(((y + j) % NY) * (2 * D) + my_row, 16)
        wy[j] = send(
            kvw.at[pl.ds(src_row, SLICE), my_cols],
            wt.at[NY - j, pl.ds(pl.multiple_of(my_row, 16), SLICE), my_cols],
            WY + n, at_y(j),
        )

    l_dec.wait()
    dg[t] = (dec_raw[...].astype(F32) * gain_ref[...]).astype(BF16)
    A, B = pl.ds(0, DHALF), pl.ds(DHALF, DHALF)
    up_a = send(dg.at[t, A], dg.at[t, A], G_UP_A, up)
    dn_b = send(dg.at[t, B], dg.at[t, B], G_DN_B, dn)
    up_b = send(dg.at[t, B], dg.at[t, B], G_UP_B, up)
    dn_a = send(dg.at[t, A], dg.at[t, A], G_DN_A, dn)
    g_core = send(dg.at[t], dg.at[t], G_CORE, core)

    ids[d] = which_ref[...]

    def send_ids(k, carry):
        remote(ids.at[d], ids.at[d], IDS, ((d + k) % NDP, t)).start()
        return carry

    lax.fori_loop(1, NDP, send_ids, 0)

    ones = jnp.ones((8, D), BF16)

    def squares(value):
        sq = value * value
        high = sq.astype(BF16)
        low = (sq - high.astype(F32)).astype(BF16)
        return nt(ones, high) + nt(ones, low)

    row8 = iota((8, 128), 0)
    l_prm.wait()
    part = jnp.zeros((8, 128), F32)
    for i in range(PR // 128):
        value = prm_raw[i * 128 : (i + 1) * 128].astype(F32)
        ps[c, i * 128 : (i + 1) * 128] = (value * gain_ref[...]).astype(BF16)
        part = jnp.where(row8 == i, squares(value), part)
    ps_copy = send(ps.at[c], ps.at[c], PS, core)
    sg[t, 0:8] = part
    part = jnp.zeros((8, 128), F32)
    for i in range(DR // 128):
        value = dec_raw[i * 128 : (i + 1) * 128].astype(F32)
        part = jnp.where(row8 == i, squares(value), part)
    sg[t, 8:16] = part
    sq = [send(sg.at[t], sg.at[t], SQ + k - 1, (d, (t + k) % NT)) for k in range(1, NT)]

    def z_piece(j):
        row = pl.multiple_of(((x % 2) * NZ + (z + NZ + j) % NZ) * SLICE, 16)
        return wt.at[pl.ds(1, NY - 1), pl.ds(row, SLICE), my_cols]

    for j in (2, 1, 3):
        wy[j].wait_recv()
    for s in range(4):
        z_up = send(z_piece(-s), z_piece(-s), WZ_UP + s, at_z(1))
        if s < 3:
            z_dn = send(z_piece(s), z_piece(s), WZ_DN + s, at_z(NZ - 1))
        z_up.wait_recv()
        if s < 3:
            z_dn.wait_recv()

    def x_piece(slot, j, first, rows):
        xx = (x + NX + j) % NX
        row = pl.multiple_of((xx % 2) * D + first, 16)
        return wt.at[slot, pl.ds(row, rows), pl.ds(pl.multiple_of((xx // 2) * 128, 128), 128)]

    x_copies = {}
    for n, slot in enumerate((2, 1, 3)):
        whole = x_piece(slot, 0, 0, D)
        x_copies[slot] = [
            send(whole, whole, WX + 4 * n, at_x(1)),
            send(whole, whole, WX + 4 * n + 1, at_x(NX - 1)),
        ]

    def x_forward(n, slot):
        x_copies[slot][0].wait_recv()
        piece = x_piece(slot, -1, 0, D // 2)
        x_copies[slot].append(send(piece, piece, WX + 4 * n + 2, at_x(1)))
        x_copies[slot][1].wait_recv()
        piece = x_piece(slot, 1, D // 2, D // 2)
        x_copies[slot].append(send(piece, piece, WX + 4 * n + 3, at_x(NX - 1)))

    def x_finish(slot):
        x_copies[slot][2].wait_recv()
        x_copies[slot][3].wait_recv()

    below, above, opposite = block_of(NY - 1), block_of(1), block_of(2)
    up_a.wait_recv()
    up_fa = send(dg.at[below, A], dg.at[below, A], G_UP_FA, up)
    dn_b.wait_recv()
    dn_fb = send(dg.at[above, B], dg.at[above, B], G_DN_FB, dn)
    relays = [
        send(dg.at[below, A], dg.at[below, A], G_REL, core),
        send(dg.at[above, B], dg.at[above, B], G_REL + 1, core),
    ]
    up_b.wait_recv()
    relays.append(send(dg.at[below, B], dg.at[below, B], G_REL + 2, core))
    dn_a.wait_recv()
    relays.append(send(dg.at[above, A], dg.at[above, A], G_REL + 3, core))

    r256, c256 = iota((DR, DR), 0), iota((DR, DR), 1)
    same = (owner_col_ref[...] == owner_row_ref[...]) & ((r256 & 3) == (c256 & 3))
    rank_row = jnp.sum(jnp.where(same & (r256 < c256), 1, 0), axis=0, keepdims=True)
    rank_col = jnp.sum(jnp.where(same & (c256 < r256), 1, 0), axis=1, keepdims=True)
    lane_row = iota((1, DR), 1)
    lane_col = iota((DR, 1), 0)
    target_row = owner_row_ref[...] * SLOTS + rank_row * 4 + (lane_row & 3)
    target_col = owner_col_ref[...] * SLOTS + rank_col * 4 + (lane_col & 3)
    n_slots = NDP * SLOTS

    up_fa.wait_recv()
    relays.append(send(dg.at[opposite, A], dg.at[opposite, A], G_REL + 4, core))
    dn_fb.wait_recv()
    relays.append(send(dg.at[opposite, B], dg.at[opposite, B], G_REL + 5, core))

    x_forward(0, 2)
    x_forward(1, 1)
    x_forward(2, 3)

    wo_copies = []
    for b in range(NY):
        cols = pl.ds(pl.multiple_of((2 * b + oc) * D, 128), D)
        wo_copies.append(send(wo_hbm.at[:, cols], wob.at[1, b], WO + b, core))

    for copy in sq:
        copy.wait_recv()
    total = sg[0]
    for k in range(1, NT):
        total = total + sg[k]
    factor = lax.rsqrt(total / MODEL_WIDTH + EPSILON)
    for i in range((PR + DR) // 128):
        rcol[i * 128 : (i + 1) * 128] = jnp.broadcast_to(factor[i : i + 1], (128, 128)).T

    g_core.wait_recv()
    for copy in relays:
        copy.wait_recv()
    l_q.wait()

    def project(k, carry):
        rows = pl.ds(pl.multiple_of(k * D, D), D)
        block = dg[k]
        add_q = nn(block, qw[rows])
        add_kv = nn(block, kvw[rows])

        @pl.when(k == 0)
        def _():
            acc[:, : GROUP * HEAD] = add_q
            acc[:, GROUP * HEAD :] = add_kv

        @pl.when(k > 0)
        def _():
            acc[:, : GROUP * HEAD] += add_q
            acc[:, GROUP * HEAD :] += add_kv

        return carry

    lax.fori_loop(0, NT, project, 0)
    scale = rcol[PR : PR + DR]
    projected = jnp.concatenate(
        [(acc[:, i * 128 : (i + 1) * 128] * scale).astype(BF16) for i in range(WIDTH // 128)], axis=1
    )
    for i in range(4):
        rows = iota((n_slots // 4, DR), 0) + i * (n_slots // 4)
        pick = jnp.where(rows == target_row, 1.0, 0.0).astype(BF16)
        placed = nn(pick, projected).astype(BF16)
        qo[i * 8 : (i + 1) * 8] = placed.reshape(8, SLOTS, WIDTH)
    qr[d] = qo[d]

    def send_q(k, carry):
        to = (d + k) % NDP
        remote(qo.at[to], qr.at[d], QX, (to, t)).start()
        return carry

    lax.fori_loop(1, NDP, send_q, 0)

    ps_copy.wait_recv()
    l_wt.wait()

    def partial(j, row, rows):
        at = pl.ds(pl.multiple_of(row, rows), rows)
        return nn(ps[0, at], wt[j, :D]) + nn(ps[1, at], wt[j, D:])

    def fill(n, j, base, extra):
        def one(i, carry):
            at = pl.ds(pl.multiple_of(i * 128, 128), 128)
            value = partial(j, base + i * 128, 128)
            if extra is not None:
                value = value + rp_recv[extra, at].astype(F32)
            rp_send[n, at] = value.astype(BF16)
            return carry

        lax.fori_loop(0, HALF // 128, one, 0)

    def rp(n, dev):
        return send(rp_send.at[n], rp_recv.at[n], RP + n, dev)

    x_finish(2)
    fill(0, 2, 0, None)
    rp0 = rp(0, dn)
    fill(1, 2, HALF, None)
    rp1 = rp(1, up)
    x_finish(1)
    fill(2, 1, 0, None)
    rp2 = rp(2, up)
    x_finish(3)
    fill(3, 3, HALF, None)
    rp3 = rp(3, dn)
    rp0.wait_recv()
    fill(4, 3, 0, 0)
    rp4 = rp(4, dn)
    rp1.wait_recv()
    fill(5, 1, HALF, 1)
    rp5 = rp(5, up)

    def own_rows(i, carry):
        at = pl.ds(pl.multiple_of(i * 128, 128), 128)
        own_sum[at] = partial(0, i * 128, 128)
        return carry

    lax.fori_loop(0, PR // 128, own_rows, 0)

    pltpu.make_async_copy(ids.at[pl.ds(0, NDP - 1)], ids.at[pl.ds(0, NDP - 1)], rs.at[IDS]).wait()
    which = jnp.concatenate([ids[s] for s in range(NDP)], axis=0)
    local = which - (PROMPTS * d).astype(F32)
    match = (local >= 0.0) & (local < float(PROMPTS))
    before = jnp.where(iota((128, 128), 0) < iota((128, 128), 1), 1.0, 0.0).astype(BF16)
    rank = nn(jnp.where(match, 1.0, 0.0).astype(BF16), before)
    lane = iota((NDP, 128), 1)
    table = jnp.zeros((NDP, 128), F32)
    for k in range(4):
        at_k = jnp.sum(
            jnp.where(match & (rank == float(k)), local, 0.0), axis=1, keepdims=True
        )
        table = jnp.where(lane == k, at_k, table)
    table = table.astype(BF16)
    for i in range(4):
        sub = iota((128, NDP), 0)
        spread = jnp.where((sub >> 4) + 8 * i == iota((128, NDP), 1), 1.0, 0.0).astype(BF16)
        wide = nn(spread, table)
        mine = iota((128, 128), 1) == ((iota((128, 128), 0) >> 2) & 3)
        pid = jnp.sum(jnp.where(mine, wide, 0.0), axis=1, keepdims=True)
        pid_ref[i * 128 : (i + 1) * 128] = jnp.broadcast_to(pid, (128, 128))
        lens = jnp.zeros((128, 1), F32)
        for p in range(PROMPTS):
            lens = jnp.where(pid == float(p), lengths_ref[PROMPTS * d + p].astype(F32), lens)
        len_ref[i * 128 : (i + 1) * 128] = jnp.broadcast_to(lens, (128, 128))

    rp2.wait_recv()
    rp4.wait_recv()

    def finish_rows(base, one_slot, two_slot):
        def one(i, carry):
            at = pl.ds(pl.multiple_of(i * 128, 128), 128)
            there = pl.ds(pl.multiple_of(base + i * 128, 128), 128)
            value = own_sum[there] + rp_recv[one_slot, at].astype(F32) + rp_recv[two_slot, at].astype(F32)
            factor = rcol[there]
            kc[there, :HEAD] = (value[:, :HEAD] * factor).astype(BF16)
            kc[there, HEAD:] = (value[:, HEAD:] * factor).astype(BF16)
            return carry

        lax.fori_loop(0, HALF // 128, one, 0)

    finish_rows(0, 2, 4)
    rp3.wait_recv()
    rp5.wait_recv()
    finish_rows(HALF, 3, 5)

    pltpu.make_async_copy(qr.at[pl.ds(0, NDP - 1)], qr.at[pl.ds(0, NDP - 1)], rs.at[QX]).wait()
    root = float(HEAD) ** -0.5

    def attend(i, carry):
        at = pl.ds(pl.multiple_of(i * 128, 128), 128)
        sources = pl.ds(pl.multiple_of(i * 8, 8), 8)
        rows = qr[sources].reshape(128, WIDTH)
        own_k = rows[:, GROUP * HEAD : GROUP * HEAD + HEAD]
        own_v = rows[:, GROUP * HEAD + HEAD :]
        pid = pid_ref[at, 0:1]
        lens = len_ref[at, 0:1]
        live = iota((128, LP), 1).astype(F32) < lens
        r, cc = iota((128, 128), 0), iota((128, 128), 1)
        usable = ((r >> 2) == (cc >> 2)) & ((cc & 3) <= (r & 3))
        results = []
        for h in range(GROUP):
            query = rows[:, h * HEAD : (h + 1) * HEAD]
            scores = nt(query, kc[0:LP, :HEAD])
            for p in range(1, PROMPTS):
                scores = jnp.where(pid == float(p), nt(query, kc[p * LP : (p + 1) * LP, :HEAD]), scores)
            scores = jnp.where(live, scores * root, HUGE_NEGATIVE)
            top = jnp.max(scores, axis=1, keepdims=True)
            weights = jnp.where(live, jnp.exp(scores - top), 0.0)
            mass = jnp.sum(weights, axis=1, keepdims=True)
            blended = jnp.zeros((128, HEAD), F32)
            for p in range(PROMPTS):
                masked = jnp.where(pid == float(p), weights, 0.0).astype(BF16)
                blended = blended + nn(masked, kc[p * LP : (p + 1) * LP, HEAD:])
            own = jnp.where(usable, nt(query, own_k) * root, HUGE_NEGATIVE)
            own_top = jnp.max(own, axis=1, keepdims=True)
            own_weights = jnp.where(usable, jnp.exp(own - own_top), 0.0)
            own_mass = jnp.sum(own_weights, axis=1, keepdims=True)
            own_blended = nn(own_weights.astype(BF16), own_v)
            highest = jnp.maximum(top, own_top)
            one, two = jnp.exp(top - highest), jnp.exp(own_top - highest)
            numerator = blended * one + own_blended * two
            denominator = mass * one + own_mass * two
            results.append((numerator / denominator).astype(BF16))
        ro_[sources] = jnp.concatenate(results, axis=1).reshape(8, SLOTS, GROUP * HEAD)
        return carry

    lax.fori_loop(0, 4, attend, 0)
    rr[d] = ro_[d]

    def send_back(k, carry):
        to = (d + k) % NDP
        remote(ro_.at[to], rr.at[d], RX, (to, t)).start()
        return carry

    lax.fori_loop(1, NDP, send_back, 0)
    pltpu.make_async_copy(rr.at[pl.ds(0, NDP - 1)], rr.at[pl.ds(0, NDP - 1)], rs.at[RX]).wait()

    take = jnp.where(iota((DR, n_slots), 1) == target_col, 1.0, 0.0).astype(BF16)
    ax[c] = nn(take, rr[...].reshape(n_slots, GROUP * HEAD)).astype(BF16)
    ax_copy = send(ax.at[c], ax.at[c], AX, core)
    for copy in l_wo:
        copy.wait()
    for copy in wo_copies:
        copy.wait_recv()
    ax_copy.wait_recv()

    def out_partial(j, row):
        b = (y + j) % NY
        at = pl.ds(row, DHALF)
        return nn(ax[c, at], wob[0, b]) + nn(ax[oc, at], wob[1, b])

    def out_send(n, j, row, extra, dev):
        value = out_partial(j, row)
        if extra is not None:
            value = value + rs_recv[extra].astype(F32)
        rs_send[n] = value.astype(BF16)
        return send(rs_send.at[n], rs_recv.at[n], RO + n, dev)

    o0 = out_send(0, 2, 0, None, dn)
    o1 = out_send(1, 2, DHALF, None, up)
    o2 = out_send(2, 1, 0, None, up)
    o3 = out_send(3, 3, DHALF, None, dn)
    o0.wait_recv()
    o4 = out_send(4, 3, 0, 0, dn)
    o1.wait_recv()
    o5 = out_send(5, 1, DHALF, 1, up)
    own_a = out_partial(0, 0)
    o2.wait_recv()
    o4.wait_recv()
    out_ref[:DHALF] = (own_a + rs_recv[2].astype(F32) + rs_recv[4].astype(F32)).astype(BF16)
    own_b = out_partial(0, DHALF)
    o3.wait_recv()
    o5.wait_recv()
    out_ref[DHALF:] = (own_b + rs_recv[3].astype(F32) + rs_recv[5].astype(F32)).astype(BF16)

    for copy in sent:
        copy.wait_send()
    for ref, n in ((ids, IDS), (qo, QX), (ro_, RX)):
        pltpu.make_async_copy(ref.at[pl.ds(0, NDP - 1)], ref.at[pl.ds(0, NDP - 1)], ss.at[n]).wait()


def shards(
    prompt_states, prompt_lengths, decode_states, sample_owner, sample_local,
    norm_gain, kv_weight, q_weight, output_weight,
):
    owner = sample_owner[:, 0]
    which = (owner * PROMPTS + sample_local).astype(F32)
    which = jnp.concatenate([which, jnp.full((64,), -1.0, F32)]).reshape(1, 128)
    owners = jnp.repeat(owner, 4)
    vmem = pl.BlockSpec(memory_space=pltpu.VMEM)
    hbm = pl.BlockSpec(memory_space=pl.ANY)
    out = pl.pallas_call(
        kernel,
        out_shape=jax.ShapeDtypeStruct((DR, D), BF16),
        in_specs=[hbm, hbm, vmem, vmem, vmem, vmem, pl.BlockSpec(memory_space=pltpu.SMEM), hbm, hbm, hbm],
        out_specs=vmem,
        scratch_shapes=[
            pltpu.VMEM((DR, D), BF16),
            pltpu.VMEM((PR, D), BF16),
            pltpu.VMEM((NT, DR, D), BF16),
            pltpu.VMEM((NC, PR, D), BF16),
            pltpu.VMEM((NT, 16, 128), F32),
            pltpu.VMEM((NDP, 1, 128), F32),
            pltpu.VMEM((MODEL_WIDTH, GROUP * HEAD), BF16),
            pltpu.VMEM((MODEL_WIDTH, 2 * HEAD), BF16),
            pltpu.VMEM((NY, 2 * D, 2 * HEAD), BF16),
            pltpu.VMEM((NC, NY, GROUP * HEAD, D), BF16),
            pltpu.VMEM((6, HALF, 2 * HEAD), BF16),
            pltpu.VMEM((6, HALF, 2 * HEAD), BF16),
            pltpu.VMEM((PR, 2 * HEAD), F32),
            pltpu.VMEM((PR, 2 * HEAD), BF16),
            pltpu.VMEM((DR, WIDTH), F32),
            pltpu.VMEM((NDP, SLOTS, WIDTH), BF16),
            pltpu.VMEM((NDP, SLOTS, WIDTH), BF16),
            pltpu.VMEM((NDP, SLOTS, GROUP * HEAD), BF16),
            pltpu.VMEM((NDP, SLOTS, GROUP * HEAD), BF16),
            pltpu.VMEM((NC, DR, GROUP * HEAD), BF16),
            pltpu.VMEM((6, DHALF, D), BF16),
            pltpu.VMEM((6, DHALF, D), BF16),
            pltpu.VMEM((NDP * SLOTS, 128), F32),
            pltpu.VMEM((NDP * SLOTS, 128), F32),
            pltpu.VMEM((PR + DR, 128), F32),
            pltpu.SemaphoreType.DMA((N_SEM,)),
            pltpu.SemaphoreType.DMA((N_SEM,)),
            pltpu.SemaphoreType.DMA((9,)),
        ],
        compiler_params=pltpu.CompilerParams(
            collective_id=0, has_side_effects=True, vmem_limit_bytes=56 * 1024 * 1024
        ),
    )(
        decode_states.reshape(DR, D),
        prompt_states.reshape(PR, D),
        norm_gain.reshape(1, D),
        which.reshape(1, 128),
        owners.reshape(1, DR),
        owners.reshape(DR, 1),
        prompt_lengths,
        kv_weight.reshape(MODEL_WIDTH, 2 * HEAD),
        q_weight.reshape(MODEL_WIDTH, GROUP * HEAD),
        output_weight.reshape(GROUP * HEAD, MODEL_WIDTH),
    )
    return out.reshape(64, 4, D)


def solution(mesh):
    placed = (
        P("dp", None, "tensor"),
        P(),
        P("dp", None, "tensor"),
        P("dp", None),
        P("dp"),
        P("tensor"),
        P(None, "tensor", None),
        P(None, "tensor", None),
        P("tensor", None, None),
    )
    return jax.shard_map(
        shards, mesh=mesh, in_specs=placed, out_specs=P("dp", None, "tensor"), check_vma=False
    )
```

time: 343 us -> 108 us (0.31)
  waiting for transfers between devices: 232 us -> 0 us
  Pallas kernels: 0 us -> 99.8 us
  matrix products: 37.4 us -> 0 us
  local copies, waits for them, and re-layouts: 30 us -> 7.53 us
  blocking collectives: 15.2 us -> 0 us
  between operations: 13.4 us -> 0.01 us
  other arithmetic: 12.6 us -> 0.68 us
    all_gather x3 -> x0, waiting for transfers between devices: 199 us -> none  [the longest x1 130 us: shards(): every_cache = lax.all_gather(prompt_cache, 'dp', axis=0, tiled=True)]
    pallas_call x0 -> x1, Pallas kernels: none -> 99.8 us  [shards(): pl.pallas_call(kernel, out_shape=jax.ShapeDtypeStruct((DR, D), BF16), in_...]
    dot_general x8 -> x0, matrix products: 37.4 us -> none  [the longest x1 8.38 us: prefix_slots(): jnp.einsum(blend_form, weights.astype(jnp.bfloat16), stored[..., head_siz...]
    unnamed x5 -> x0, waiting for transfers between devices: 32.2 us -> none
    unnamed x12 -> x0, local copies, waits for them, and re-layouts: 17.1 us -> none
    psum x1 -> x0, blocking collectives: 15.2 us -> none  [shards(): lax.psum((jnp.sum(prompt_wide * prompt_wide, axis=-1), jnp.sum(decode_wid...]
    reduce_sum x4 -> x0, other arithmetic: 9.96 us -> none  [the longest x1 6.46 us: prefix_slots(): weight_sum = jnp.sum(weights, axis=(-2, -1))]
    reshape x2 -> x4, local copies, waits for them, and re-layouts: 0.32 us -> 5.36 us  [the longest x1 1.78 us: shards(): return out.reshape(64, 4, D)]
  transfers between devices with their start and end apart: 4 -> 0, of which waited for: 4 -> 0; matrix products, arithmetic and copies ran while one was open for 7% -> 0% of each run, Pallas kernels for 0% -> 0%
where the time goes in v1:
time: 108 us
  Pallas kernels  99.8 us (92%)
  local copies, waits for them, and re-layouts  7.53 us (7%)
    pallas_call x1, Pallas kernels, shards(): pl.pallas_call(kernel, out_shape=jax.ShapeDtypeStruct((DR, D), BF16), in_...  99.8 us

profile of v1, /device:TPU:1, one launch (start us, length us, event | category | flops | bytes accessed | tf_op | source)
XLA Modules:
  0.0 108.1 jit_solution(4990803924767053861)
XLA Ops:
  0.0 0.7 add_convert_fusion
  0.7 0.5 pad_bitcast_fusion.which_ref
  1.2 1.3 %reshape.26.gain_ref = f32[1,640]{1,0:T(1,128)} reshape(f32[640]{0:T(1024)} %param.14) | data formatting | bytes 5120 | tf_op jit(solution)/shard_map/reshape | solution.py:556
  2.5 0.7 broadcast_in_dim.4
  3.2 0.7 reshape_reshape.6.owner_row_ref
  3.9 0.7 reshape_reshape.8.owner_col_ref
  4.7 1.8 %reshape.24.decode_hbm = bf16[256,640]{1,0:T(8,128)(2,1)} reshape(bf16[64,4,640]{2,1,0:T(4,128)(2,1)} %param.11) | data formatting | bytes 655360 | tf_op jit(solution)/shard_map/reshape | solution.py:554
  6.4 99.8 %shard_map.91 = bf16[256,640]{1,0:T(8,128)(2,1)} custom-call(bf16[256,640]{1,0:T(8,128)(2,1)} %reshape.24.decode_hbm, bf16[1024,640]{1,0:T(8,128)(2,1)} %bitcast.11, f32[1,640]{1,0:T(1,128)} %reshape.26.gain_ref, f32[1,128]{1,0:T(1,128)} %pad_bitcast_fusion.which_ref, s32[1,256]{1,0:T(1,128)} %reshape_reshape.6.owner_row_ref, ...), custom_call_target="tpu_custom_call" | custom-call | tf_op jit(solution)/shard_map/pallas_call | solution.py:515
  106.3 1.8 %reshape.31 = bf16[64,4,640]{2,1,0:T(4,128)(2,1)} reshape(bf16[256,640]{1,0:T(8,128)(2,1)} %shard_map.91) | data formatting | bytes 655360 | tf_op jit(solution)/shard_map/reshape | solution.py:565

commit v2 on v1

v2 whole, which is shorter than its diff:
```python
import jax
import jax.numpy as jnp
from jax import lax
from jax.experimental import pallas as pl
from jax.experimental.pallas import tpu as pltpu
from jax.sharding import PartitionSpec as P

MESH = pl.DeviceIdType.MESH
F32 = jnp.float32
BF16 = jnp.bfloat16

MODEL_WIDTH = 5120
EPSILON = 1e-06
HUGE_NEGATIVE = -1e30

NX, NZ, NY, NC = 4, 8, 4, 2
NDP = NX * NZ
NT = NY * NC
D = 640
HEAD = 128
GROUP = 3
PROMPTS = 4
LP = 256
PR = PROMPTS * LP
HALF = PR // 2
DR = 256
DHALF = DR // 2
SLOTS = 16
WIDTH = GROUP * HEAD + 2 * HEAD
SLICE = 80

A_ROWS = 48

IDS, QX, RX = 0, 1, 2
N_SEM = 160


def nn(a, b):
    return lax.dot_general(a, b, (((1,), (0,)), ((), ())), preferred_element_type=F32)


def nt(a, b):
    return lax.dot_general(a, b, (((1,), (1,)), ((), ())), preferred_element_type=F32)


def iota(shape, dim):
    return lax.broadcasted_iota(jnp.int32, shape, dim)


def kernel(
    decode_hbm, prompt_hbm, gain_ref, owner_ref, local_ref, lengths_ref,
    kv_hbm, q_hbm, wo_hbm,
    out_ref,
    dec_raw, prm_raw, dg, ps, sg, ids, qw, kvw, wt, wob,
    rp_send, rp_recv, own_sum, kt, vc, acc, qo, qr, ro_, rr, ax, rs_send, rs_recv,
    pid_ref, len_ref, rcol,
    ss, rs, ls,
):
    d = lax.axis_index("dp")
    t = lax.axis_index("tensor")
    z, x = d // NX, d % NX
    y, c = t // NC, t % NC
    oc = 1 - c

    def at_y(j):
        return (d, ((y + j) % NY) * NC + c)

    def at_z(j):
        return (((z + j) % NZ) * NX + x, t)

    def at_x(j):
        return (z * NX + (x + j) % NX, t)

    core = (d, y * NC + oc)
    up, dn = at_y(1), at_y(NY - 1)

    def block_of(j):
        return ((y + j) % NY) * NC + c

    def remote(src, dst, n, dev):
        return pltpu.make_async_remote_copy(
            src_ref=src, dst_ref=dst, send_sem=ss.at[n], recv_sem=rs.at[n],
            device_id=dev, device_id_type=MESH,
        )

    sent = []

    def send(src, dst, dev):
        copy = remote(src, dst, 3 + len(sent), dev)
        copy.start()
        sent.append(copy)
        return copy

    def local_copy(src, dst, n):
        copy = pltpu.make_async_copy(src, dst, ls.at[n])
        copy.start()
        return copy

    def many(ref, sem):
        part = ref.at[pl.ds(0, NDP - 1)]
        return pltpu.make_async_copy(part, part, sem)

    def send_many(ref, to_ref, n, per_target):
        def one(k, carry):
            to = (d + k) % NDP
            remote(ref.at[to if per_target else d], to_ref.at[d], n, (to, t)).start()
            return carry

        lax.fori_loop(1, NDP, one, 0)

    def wait_many(to_ref, n):
        many(to_ref, rs.at[n]).wait()

    l_dec = local_copy(decode_hbm, dec_raw, 0)
    l_kv = local_copy(kv_hbm, kvw, 2)
    l_prm = local_copy(prompt_hbm, prm_raw, 1)
    l_q = local_copy(q_hbm, qw, 3)
    l_wt = local_copy(kv_hbm.at[y], wt.at[0], 4)
    l_wo = []
    for b in range(NY):
        cols = pl.ds(pl.multiple_of((2 * b + c) * D, 128), D)
        l_wo.append(local_copy(wo_hbm.at[:, cols], wob.at[0, b], 5 + b))

    barrier = pltpu.get_barrier_semaphore()
    for k in range(1, NT):
        pl.semaphore_signal(barrier, inc=1, device_id=(d, (t + k) % NT), device_id_type=MESH)

    def greet(k, carry):
        pl.semaphore_signal(barrier, inc=1, device_id=((d + k) % NDP, t), device_id_type=MESH)
        return carry

    lax.fori_loop(1, NDP, greet, 0)
    pl.semaphore_wait(barrier, NT - 1 + NDP - 1)

    xb, my_cols = x % 2, pl.ds(pl.multiple_of((x // 2) * 128, 128), 128)
    slots = (2, 1, 3)
    wy = {}
    for j in slots:
        wy[j] = send(
            kv_hbm.at[(y + j) % NY, xb, z, :, my_cols], wt.at[NY - j, xb, z, :, my_cols], at_y(j)
        )
    arrives = {j: wy[NY - j] for j in slots}

    l_dec.wait()
    gain = gain_ref[...].reshape(1, D)
    decode = dec_raw[...].astype(F32).reshape(DR, D)
    dg[t] = (decode * gain).astype(BF16)
    A, B = pl.ds(0, DHALF), pl.ds(DHALF, DHALF)

    def block(k, rows, dev):
        return send(dg.at[k, rows], dg.at[k, rows], dev)

    up_a = block(t, A, up)
    dn_b = block(t, B, dn)
    up_b = block(t, B, up)
    dn_a = block(t, A, dn)
    g_core = send(dg.at[t], dg.at[t], core)

    def same(ref, dev):
        return send(ref, ref, dev)

    up_z, dn_z, up_x, dn_x = at_z(1), at_z(NZ - 1), at_x(1), at_x(NX - 1)

    def a_piece(slot, j, first=0, rows=A_ROWS):
        return wt.at[slot, xb, (z + NZ + j) % NZ, pl.ds(first, rows), my_cols]

    def b_piece(slot, j, first=A_ROWS, rows=SLICE - A_ROWS):
        return wt.at[slot, :, (z + NZ + j) % NZ, pl.ds(first, rows)]

    def x_piece(slot, j, zs, rows):
        xx = (x + NX + j) % NX
        cols = pl.ds(pl.multiple_of((xx // 2) * 128, 128), 128)
        return wt.at[slot, xx % 2, zs, rows, cols]

    here = pl.ds(z, 1)
    a_rows, b_rows = pl.ds(0, A_ROWS), pl.ds(A_ROWS, SLICE - A_ROWS)
    b_mid = A_ROWS + (SLICE - A_ROWS) // 2
    az, ax_, bz, bx = {}, {}, {}, {}
    for slot in slots:
        arrives[slot].wait_recv()
        az[slot] = same(a_piece(slot, 0), up_z), same(a_piece(slot, 0), dn_z)
        piece = x_piece(slot, 0, here, b_rows)
        bx[slot] = same(piece, up_x), same(piece, dn_x)

    def a_step(slot, step):
        az[slot][0].wait_recv()
        az[slot][1].wait_recv()
        if step < 3:
            az[slot] = same(a_piece(slot, -step), up_z), same(a_piece(slot, step), dn_z)
        elif step == 3:
            az[slot] = (
                same(a_piece(slot, -3, 0, 32), up_z), same(a_piece(slot, 3, 32, A_ROWS - 32), dn_z)
            )

    def b_step(slot, step):
        bz[slot][0].wait_recv()
        bz[slot][1].wait_recv()
        if step < 3:
            bz[slot] = same(b_piece(slot, -step), up_z), same(b_piece(slot, step), dn_z)
        elif step == 3:
            bz[slot] = (
                same(b_piece(slot, -3, A_ROWS, b_mid - A_ROWS), up_z),
                same(b_piece(slot, 3, b_mid, SLICE - b_mid), dn_z),
            )

    mine = (owner_ref[...] * PROMPTS + local_ref[...]).astype(F32)
    ids[d] = jnp.concatenate([mine, jnp.full((1, 64), -1.0, F32)], axis=1)
    send_many(ids, ids, IDS, False)

    ones = jnp.ones((8, D), BF16)

    def squares(value):
        sq = value * value
        high = sq.astype(BF16)
        low = (sq - high.astype(F32)).astype(BF16)
        return nt(ones, high) + nt(ones, low)

    row8 = iota((8, 128), 0)
    parts = [jnp.zeros((8, 128), F32)]

    def prompt_block(i):
        value = prm_raw[i * 128 : (i + 1) * 128].astype(F32)
        ps[c, i * 128 : (i + 1) * 128] = (value * gain).astype(BF16)
        parts[0] = jnp.where(row8 == i, squares(value), parts[0])

    l_prm.wait()
    prompt_block(0)
    prompt_block(1)
    for slot in slots:
        a_step(slot, 1)
        bx[slot][0].wait_recv()
        bx[slot][1].wait_recv()
        bx[slot] = (
            same(x_piece(slot, -1, here, pl.ds(A_ROWS, b_mid - A_ROWS)), up_x),
            same(x_piece(slot, 1, here, pl.ds(b_mid, SLICE - b_mid)), dn_x),
        )
    prompt_block(2)
    prompt_block(3)
    for slot in slots:
        a_step(slot, 2)
        bx[slot][0].wait_recv()
        bx[slot][1].wait_recv()
        bz[slot] = same(b_piece(slot, 0), up_z), same(b_piece(slot, 0), dn_z)
    prompt_block(4)
    prompt_block(5)

    below, above, opposite = block_of(NY - 1), block_of(1), block_of(2)
    up_a.wait_recv()
    up_fa = block(below, A, up)
    dn_b.wait_recv()
    dn_fb = block(above, B, dn)
    relays = [block(below, A, core), block(above, B, core)]
    prompt_block(6)
    prompt_block(7)
    ps_copy = same(ps.at[c], core)
    sg[t, 0:8] = parts[0]
    part = jnp.zeros((8, 128), F32)
    for i in range(DR // 128):
        part = jnp.where(row8 == i, squares(decode[i * 128 : (i + 1) * 128]), part)
    sg[t, 8:16] = part
    sq = [same(sg.at[t], (d, (t + k) % NT)) for k in range(1, NT)]

    for slot in slots:
        a_step(slot, 3)
        b_step(slot, 1)
    up_b.wait_recv()
    relays.append(block(below, B, core))
    dn_a.wait_recv()
    relays.append(block(above, A, core))

    l_q.wait()
    l_kv.wait()

    def project(k, first=False):
        add_q = nn(dg[k], qw[k])
        add_kv = nn(dg[k], kvw[k // 2, k % 2].reshape(D, 2 * HEAD))
        if first:
            acc[:, : GROUP * HEAD] = add_q
            acc[:, GROUP * HEAD :] = add_kv
        else:
            acc[:, : GROUP * HEAD] += add_q
            acc[:, GROUP * HEAD :] += add_kv

    project(t, True)
    for slot in slots:
        a_step(slot, 4)
        whole = x_piece(slot, 0, pl.ds(0, NZ), a_rows)
        ax_[slot] = same(whole, up_x), same(whole, dn_x)
        b_step(slot, 2)
    project(below)
    project(above)
    up_fa.wait_recv()
    relays.append(block(opposite, A, core))
    dn_fb.wait_recv()
    relays.append(block(opposite, B, core))
    for slot in slots:
        ax_[slot][0].wait_recv()
        ax_[slot][1].wait_recv()
        ax_[slot] = (
            same(x_piece(slot, -1, pl.ds(0, NZ // 2), a_rows), up_x),
            same(x_piece(slot, 1, pl.ds(NZ // 2, NZ // 2), a_rows), dn_x),
        )
        b_step(slot, 3)

    def slot_ready(slot):
        ax_[slot][0].wait_recv()
        ax_[slot][1].wait_recv()
        b_step(slot, 4)

    project(opposite)
    g_core.wait_recv()
    for copy in relays:
        copy.wait_recv()
    for j in range(NY):
        project(((y + j) % NY) * NC + oc)

    r256, c256 = iota((DR, DR), 0), iota((DR, DR), 1)
    owners = jnp.broadcast_to(owner_ref[...].astype(F32), (8, 64)).astype(BF16)
    spread = jnp.where(iota((64, DR), 0) == (iota((64, DR), 1) >> 2), 1.0, 0.0).astype(BF16)
    owner_row = nn(owners, spread)[0:1].astype(jnp.int32)
    spread = jnp.where((iota((DR, 64), 0) >> 2) == iota((DR, 64), 1), 1.0, 0.0).astype(BF16)
    owner_col = nt(spread, owners)[:, 0:1].astype(jnp.int32)
    alike = (owner_col == owner_row) & ((r256 & 3) == (c256 & 3))
    rank_row = jnp.sum(jnp.where(alike & (r256 < c256), 1, 0), axis=0, keepdims=True)
    rank_col = jnp.sum(jnp.where(alike & (c256 < r256), 1, 0), axis=1, keepdims=True)
    lane_row = iota((1, DR), 1)
    lane_col = iota((DR, 1), 0)
    target_row = owner_row * SLOTS + rank_row * 4 + (lane_row & 3)
    target_col = owner_col * SLOTS + rank_col * 4 + (lane_col & 3)
    n_slots = NDP * SLOTS

    for copy in sq:
        copy.wait_recv()
    total = sg[0]
    for k in range(1, NT):
        total = total + sg[k]
    factor = lax.rsqrt(total / MODEL_WIDTH + EPSILON)
    for i in range((PR + DR) // 128):
        rcol[i * 128 : (i + 1) * 128] = jnp.broadcast_to(factor[i : i + 1], (128, 128)).T

    scale = rcol[PR : PR + DR]
    projected = jnp.concatenate(
        [(acc[:, i * 128 : (i + 1) * 128] * scale).astype(BF16) for i in range(WIDTH // 128)], axis=1
    )
    for i in range(4):
        rows = iota((n_slots // 4, DR), 0) + i * (n_slots // 4)
        pick = jnp.where(rows == target_row, 1.0, 0.0).astype(BF16)
        placed = nn(pick, projected).astype(BF16)
        qo[i * 8 : (i + 1) * 8] = placed.reshape(8, SLOTS, WIDTH)
    qr[d] = qo[d]
    send_many(qo, qr, QX, True)

    ps_copy.wait_recv()
    l_wt.wait()

    def partial(j, row, rows):
        at = pl.ds(pl.multiple_of(row, rows), rows)
        return nn(ps[0, at], wt[j, 0].reshape(D, 2 * HEAD)) + nn(ps[1, at], wt[j, 1].reshape(D, 2 * HEAD))

    def fill(n, j, base, extra):
        def one(i, carry):
            at = pl.ds(pl.multiple_of(i * 128, 128), 128)
            value = partial(j, base + i * 128, 128)
            if extra is not None:
                value = value + rp_recv[extra, at].astype(F32)
            rp_send[n, at] = value.astype(BF16)
            return carry

        lax.fori_loop(0, HALF // 128, one, 0)

    def rp(n, dev):
        return send(rp_send.at[n], rp_recv.at[n], dev)

    slot_ready(2)
    fill(0, 2, 0, None)
    rp0 = rp(0, dn)
    fill(1, 2, HALF, None)
    rp1 = rp(1, up)
    slot_ready(1)
    fill(2, 1, 0, None)
    rp2 = rp(2, up)
    slot_ready(3)
    fill(3, 3, HALF, None)
    rp3 = rp(3, dn)
    rp0.wait_recv()
    fill(4, 3, 0, 0)
    rp4 = rp(4, dn)
    rp1.wait_recv()
    fill(5, 1, HALF, 1)
    rp5 = rp(5, up)

    def own_rows(i, carry):
        at = pl.ds(pl.multiple_of(i * 128, 128), 128)
        own_sum[at] = partial(0, i * 128, 128)
        return carry

    lax.fori_loop(0, PR // 128, own_rows, 0)

    wo_copies = []
    for b in range(NY):
        cols = pl.ds(pl.multiple_of((2 * b + oc) * D, 128), D)
        wo_copies.append(send(wo_hbm.at[:, cols], wob.at[1, b], core))

    wait_many(ids, IDS)
    which = jnp.concatenate([ids[s] for s in range(NDP)], axis=0)
    local = which - (PROMPTS * d).astype(F32)
    match = (local >= 0.0) & (local < float(PROMPTS))
    before = jnp.where(iota((128, 128), 0) < iota((128, 128), 1), 1.0, 0.0).astype(BF16)
    rank = nn(jnp.where(match, 1.0, 0.0).astype(BF16), before)
    lane = iota((NDP, 128), 1)
    table = jnp.zeros((NDP, 128), F32)
    for k in range(4):
        at_k = jnp.sum(
            jnp.where(match & (rank == float(k)), local, 0.0), axis=1, keepdims=True
        )
        table = jnp.where(lane == k, at_k, table)
    table = table.astype(BF16)
    for i in range(4):
        sub = iota((128, NDP), 0)
        spread = jnp.where((sub >> 4) + 8 * i == iota((128, NDP), 1), 1.0, 0.0).astype(BF16)
        wide = nn(spread, table)
        mine = iota((128, 128), 1) == ((iota((128, 128), 0) >> 2) & 3)
        pid = jnp.sum(jnp.where(mine, wide, 0.0), axis=1, keepdims=True)
        pid_ref[i * 128 : (i + 1) * 128] = jnp.broadcast_to(pid, (128, 128))
        lens = jnp.zeros((128, 1), F32)
        for p in range(PROMPTS):
            lens = jnp.where(pid == float(p), lengths_ref[PROMPTS * d + p].astype(F32), lens)
        len_ref[i * 128 : (i + 1) * 128] = jnp.broadcast_to(lens, (128, 128))

    rp2.wait_recv()
    rp4.wait_recv()

    def finish_rows(base, one_slot, two_slot):
        def one(i, carry):
            at = pl.ds(pl.multiple_of(i * 128, 128), 128)
            there = pl.ds(pl.multiple_of(base + i * 128, 128), 128)
            value = own_sum[there] + rp_recv[one_slot, at].astype(F32) + rp_recv[two_slot, at].astype(F32)
            factor = rcol[there]
            kt[base // 128 + i] = (value[:, :HEAD] * factor).T.astype(BF16)
            vc[there] = (value[:, HEAD:] * factor).astype(BF16)
            return carry

        lax.fori_loop(0, HALF // 128, one, 0)

    finish_rows(0, 2, 4)
    rp3.wait_recv()
    rp5.wait_recv()
    finish_rows(HALF, 3, 5)

    wait_many(qr, QX)
    root = float(HEAD) ** -0.5
    rows3 = GROUP * 128

    def thrice(value):
        return jnp.concatenate([value] * GROUP, axis=0)

    def attend(step, carry):
        i = (z // 2 + step) % 4
        at = pl.ds(pl.multiple_of(i * 128, 128), 128)
        sources = pl.ds(pl.multiple_of(i * 8, 8), 8)
        rows = qr[sources].reshape(128, WIDTH)
        own_k = rows[:, GROUP * HEAD : GROUP * HEAD + HEAD]
        own_v = rows[:, GROUP * HEAD + HEAD :]
        pid = thrice(pid_ref[at, 0:1])
        lens = thrice(len_ref[at, 0:1])
        live = iota((rows3, LP), 1).astype(F32) < lens
        r, cc = iota((rows3, 128), 0) & 127, iota((rows3, 128), 1)
        usable = ((r >> 2) == (cc >> 2)) & ((cc & 3) <= (r & 3))
        query = jnp.concatenate([rows[:, h * HEAD : (h + 1) * HEAD] for h in range(GROUP)], axis=0)
        scores = None
        for p in range(PROMPTS):
            keys = jnp.concatenate([kt[2 * p], kt[2 * p + 1]], axis=1)
            found = nn(query, keys)
            scores = found if p == 0 else jnp.where(pid == float(p), found, scores)
        scores = jnp.where(live, scores * root, HUGE_NEGATIVE)
        top = jnp.max(scores, axis=1, keepdims=True)
        weights = jnp.where(live, jnp.exp(scores - top), 0.0)
        mass = jnp.sum(weights, axis=1, keepdims=True)
        blended = jnp.zeros((rows3, HEAD), F32)
        for p in range(PROMPTS):
            masked = jnp.where(pid == float(p), weights, 0.0).astype(BF16)
            blended = blended + nn(masked, vc[p * LP : (p + 1) * LP])
        own = jnp.where(usable, nt(query, own_k) * root, HUGE_NEGATIVE)
        own_top = jnp.max(own, axis=1, keepdims=True)
        own_weights = jnp.where(usable, jnp.exp(own - own_top), 0.0)
        own_mass = jnp.sum(own_weights, axis=1, keepdims=True)
        own_blended = nn(own_weights.astype(BF16), own_v)
        highest = jnp.maximum(top, own_top)
        one, two = jnp.exp(top - highest), jnp.exp(own_top - highest)
        numerator = blended * one + own_blended * two
        denominator = mass * one + own_mass * two
        result = (numerator / denominator).astype(BF16)
        result = jnp.concatenate([result[h * 128 : (h + 1) * 128] for h in range(GROUP)], axis=1)
        ro_[sources] = result.reshape(8, SLOTS, GROUP * HEAD)

        def give(k, carry):
            to = i * 8 + k

            @pl.when(to != d)
            def _():
                remote(ro_.at[to], rr.at[d], RX, (to, t)).start()

            return carry

        lax.fori_loop(0, 8, give, 0)
        return carry

    lax.fori_loop(0, 4, attend, 0)
    rr[d] = ro_[d]
    wait_many(rr, RX)

    take = jnp.where(iota((DR, n_slots), 1) == target_col, 1.0, 0.0).astype(BF16)
    ax[c] = nn(take, rr[...].reshape(n_slots, GROUP * HEAD)).astype(BF16)
    ax_copy = same(ax.at[c], core)
    for copy in l_wo:
        copy.wait()
    for copy in wo_copies:
        copy.wait_recv()
    ax_copy.wait_recv()

    def out_partial(j, row):
        b = (y + j) % NY
        at = pl.ds(row, DHALF)
        return nn(ax[c, at], wob[0, b]) + nn(ax[oc, at], wob[1, b])

    def out_send(n, j, row, extra, dev):
        value = out_partial(j, row)
        if extra is not None:
            value = value + rs_recv[extra].astype(F32)
        rs_send[n] = value.astype(BF16)
        return send(rs_send.at[n], rs_recv.at[n], dev)

    o0 = out_send(0, 2, 0, None, dn)
    o1 = out_send(1, 2, DHALF, None, up)
    o2 = out_send(2, 1, 0, None, up)
    o3 = out_send(3, 3, DHALF, None, dn)
    o0.wait_recv()
    o4 = out_send(4, 3, 0, 0, dn)
    o1.wait_recv()
    o5 = out_send(5, 1, DHALF, 1, up)
    own_a = out_partial(0, 0)
    o2.wait_recv()
    o4.wait_recv()
    own_a = own_a + rs_recv[2].astype(F32) + rs_recv[4].astype(F32)
    out_ref[: DHALF // 4] = own_a.reshape(DHALF // 4, 4, D).astype(BF16)
    own_b = out_partial(0, DHALF)
    o3.wait_recv()
    o5.wait_recv()
    own_b = own_b + rs_recv[3].astype(F32) + rs_recv[5].astype(F32)
    out_ref[DHALF // 4 :] = own_b.reshape(DHALF // 4, 4, D).astype(BF16)

    for copy in sent:
        copy.wait_send()
    for ref, n in ((ids, IDS), (qo, QX), (ro_, RX)):
        many(ref, ss.at[n]).wait()


def shards(
    prompt_states, prompt_lengths, decode_states, sample_owner, sample_local,
    norm_gain, kv_weight, q_weight, output_weight,
):
    vmem = pl.BlockSpec(memory_space=pltpu.VMEM)
    hbm = pl.BlockSpec(memory_space=pl.ANY)
    out = pl.pallas_call(
        kernel,
        out_shape=jax.ShapeDtypeStruct((DR // 4, 4, D), BF16),
        in_specs=[hbm, hbm, vmem, vmem, vmem, pl.BlockSpec(memory_space=pltpu.SMEM), hbm, hbm, hbm],
        out_specs=vmem,
        scratch_shapes=[
            pltpu.VMEM((DR // 4, 4, D), BF16),
            pltpu.VMEM((PR, D), BF16),
            pltpu.VMEM((NT, DR, D), BF16),
            pltpu.VMEM((NC, PR, D), BF16),
            pltpu.VMEM((NT, 16, 128), F32),
            pltpu.VMEM((NDP, 1, 128), F32),
            pltpu.VMEM((NT, D, GROUP * HEAD), BF16),
            pltpu.VMEM((NY, 2, NZ, SLICE, 2 * HEAD), BF16),
            pltpu.VMEM((NY, 2, NZ, SLICE, 2 * HEAD), BF16),
            pltpu.VMEM((NC, NY, GROUP * HEAD, D), BF16),
            pltpu.VMEM((6, HALF, 2 * HEAD), BF16),
            pltpu.VMEM((6, HALF, 2 * HEAD), BF16),
            pltpu.VMEM((PR, 2 * HEAD), F32),
            pltpu.VMEM((PR // 128, HEAD, 128), BF16),
            pltpu.VMEM((PR, HEAD), BF16),
            pltpu.VMEM((DR, WIDTH), F32),
            pltpu.VMEM((NDP, SLOTS, WIDTH), BF16),
            pltpu.VMEM((NDP, SLOTS, WIDTH), BF16),
            pltpu.VMEM((NDP, SLOTS, GROUP * HEAD), BF16),
            pltpu.VMEM((NDP, SLOTS, GROUP * HEAD), BF16),
            pltpu.VMEM((NC, DR, GROUP * HEAD), BF16),
            pltpu.VMEM((6, DHALF, D), BF16),
            pltpu.VMEM((6, DHALF, D), BF16),
            pltpu.VMEM((NDP * SLOTS, 128), F32),
            pltpu.VMEM((NDP * SLOTS, 128), F32),
            pltpu.VMEM((PR + DR, 128), F32),
            pltpu.SemaphoreType.DMA((N_SEM,)),
            pltpu.SemaphoreType.DMA((N_SEM,)),
            pltpu.SemaphoreType.DMA((9,)),
        ],
        compiler_params=pltpu.CompilerParams(
            collective_id=0, has_side_effects=True, vmem_limit_bytes=56 * 1024 * 1024
        ),
    )(
        decode_states,
        prompt_states.reshape(PR, D),
        norm_gain,
        sample_owner.reshape(1, 64),
        sample_local.reshape(1, 64),
        prompt_lengths,
        kv_weight.reshape(NY, 2, NZ, SLICE, 2 * HEAD),
        q_weight.reshape(NT, D, GROUP * HEAD),
        output_weight.reshape(GROUP * HEAD, MODEL_WIDTH),
    )
    return out


def solution(mesh):
    placed = (
        P("dp", None, "tensor"),
        P(),
        P("dp", None, "tensor"),
        P("dp", None),
        P("dp"),
        P("tensor"),
        P(None, "tensor", None),
        P(None, "tensor", None),
        P("tensor", None, None),
    )
    return jax.shard_map(
        shards, mesh=mesh, in_specs=placed, out_specs=P("dp", None, "tensor"), check_vma=False
    )
```

time: 108 us -> 90.1 us (0.83)
  Pallas kernels: 99.8 us -> 88.1 us
  local copies, waits for them, and re-layouts: 7.53 us -> 1.81 us
    pallas_call x1, Pallas kernels: 99.8 us -> 88.1 us  [shards(): pl.pallas_call(kernel, out_shape=jax.ShapeDtypeStruct((DR // 4, 4, D), BF...]
    reshape x4 -> x0, local copies, waits for them, and re-layouts: 5.36 us -> none  [the longest x1 1.78 us: shards(): return out.reshape(64, 4, D)]
    unnamed x0 -> x1, local copies, waits for them, and re-layouts: none -> 1.81 us
    another operation x2 -> x0, local copies, waits for them, and re-layouts: 1.45 us -> none  [the longest x1 0.74 us: shards(): owners.reshape(DR, 1)]
where the time goes in v2:
time: 90.1 us; the launch traced here: 89.9 us
  Pallas kernels  88.1 us (98%)
  local copies, waits for them, and re-layouts  1.81 us (2%)
    pallas_call x1, Pallas kernels, shards(): pl.pallas_call(kernel, out_shape=jax.ShapeDtypeStruct((DR // 4, 4, D), BF...  88.1 us
    unnamed x1, local copies, waits for them, and re-layouts  1.81 us

profile of v2, /device:TPU:1, one launch (start us, length us, event | category | flops | bytes accessed | tf_op | source)
XLA Modules:
  0.0 89.9 jit_solution(6418593382929346834)
XLA Ops:
  0.0 88.1 %shard_map.91 = bf16[64,4,640]{2,1,0:T(4,128)(2,1)} custom-call(bf16[64,4,640]{2,1,0:T(4,128)(2,1)} %decode_hbm.1, bf16[1024,640]{1,0:T(8,128)(2,1)} %bitcast.9, f32[640]{0:T(1024)} %gain_ref.1, s32[1,64]{1,0:T(1,128)} %bitcast.10, s32[1,64]{1,0:T(1,128)} %bitcast.11, s32[128]{0:T(128)} %lengths_ref.1, bf16[4,2,8,80,256]{4,3,2,1,0:T(8,128)(2,1)} %bitcast.8, ...), custom_call_target="tpu_custom_call" | custom-call | tf_op jit(solution)/shard_map/pallas_call | solution.py:564
  88.1 1.8 %copy.11 = bf16[64,4,640]{2,1,0:T(4,128)(2,1)} copy(bf16[64,4,640]{2,1,0:T(4,128)(2,1)} %shard_map.91) | data formatting | bytes 655360

commit v3 on v2

v3 whole, which is shorter than its diff:
```python
import jax
import jax.numpy as jnp
from jax import lax
from jax.experimental import pallas as pl
from jax.experimental.pallas import tpu as pltpu
from jax.sharding import PartitionSpec as P

MESH = pl.DeviceIdType.MESH
F32 = jnp.float32
BF16 = jnp.bfloat16

MODEL_WIDTH = 5120
EPSILON = 1e-06
HUGE_NEGATIVE = -1e30

NX, NZ, NY, NC = 4, 8, 4, 2
NDP = NX * NZ
NT = NY * NC
D = 640
HEAD = 128
GROUP = 3
PROMPTS = 4
LP = 256
PR = PROMPTS * LP
HALF = PR // 2
DR = 256
DHALF = DR // 2
SLOTS = 16
WIDTH = GROUP * HEAD + 2 * HEAD

Z_ROWS, X_ROWS = 48, 224

IDS, QX, RX, LX = 0, 1, 2, 3
N_SEM = 160


def nn(a, b):
    return lax.dot_general(a, b, (((1,), (0,)), ((), ())), preferred_element_type=F32)


def nt(a, b):
    return lax.dot_general(a, b, (((1,), (1,)), ((), ())), preferred_element_type=F32)


def exact(a, b):
    return lax.dot_general(
        a, b, (((1,), (0,)), ((), ())), precision=lax.Precision.HIGHEST, preferred_element_type=F32
    )


def iota(shape, dim):
    return lax.broadcasted_iota(jnp.int32, shape, dim)


def kernel(
    decode_hbm, prompt_hbm, gain_hbm, owner_hbm, local_hbm, lengths_hbm,
    kv_hbm, q_hbm, wo_hbm,
    out_hbm,
    gain_ref, owner_ref, local_ref, lengths_ref, out_ref, dec_raw, prm_raw, dg, ps, sg, ids, qw, kvw, wt, wob,
    rp_send, rp_recv, own_sum, kt, vc, acc, pj, qo, qr, lo, lr, mine_ref, ro_, rr, ax, rs_send, rs_recv,
    pid_ref, len_ref, rcol,
    ss, rs, ls,
):
    d = lax.axis_index("dp")
    t = lax.axis_index("tensor")
    z, x = d // NX, d % NX
    y, c = t // NC, t % NC
    oc = 1 - c

    def at_y(j):
        return (d, ((y + j) % NY) * NC + c)

    def at_z(j):
        return (((z + j) % NZ) * NX + x, t)

    def at_x(j):
        return (z * NX + (x + j) % NX, t)

    core = (d, y * NC + oc)
    up, dn = at_y(1), at_y(NY - 1)

    def block_of(j):
        return ((y + j) % NY) * NC + c

    def remote(src, dst, n, dev):
        return pltpu.make_async_remote_copy(
            src_ref=src, dst_ref=dst, send_sem=ss.at[n], recv_sem=rs.at[n],
            device_id=dev, device_id_type=MESH,
        )

    sent = []

    def send(src, dst, dev):
        copy = remote(src, dst, 4 + len(sent), dev)
        copy.start()
        sent.append(copy)
        return copy

    def local_copy(src, dst, n):
        copy = pltpu.make_async_copy(src, dst, ls.at[n])
        copy.start()
        return copy

    def many(ref, sem):
        part = ref.at[pl.ds(0, NDP - 1)]
        return pltpu.make_async_copy(part, part, sem)

    def send_many(ref, to_ref, n, per_target):
        def one(k, carry):
            to = (d + k) % NDP
            remote(ref.at[to if per_target else d], to_ref.at[d], n, (to, t)).start()
            return carry

        lax.fori_loop(1, NDP, one, 0)

    def wait_many(to_ref, n):
        many(to_ref, rs.at[n]).wait()

    l_dec = local_copy(decode_hbm, dec_raw, 0)
    l_gain = local_copy(gain_hbm, gain_ref, 9)
    l_owner = local_copy(owner_hbm, owner_ref, 10)
    l_local = local_copy(local_hbm, local_ref, 11)
    l_prm = local_copy(prompt_hbm, prm_raw, 1)
    l_lengths = local_copy(lengths_hbm, lengths_ref, 12)

    barrier = pltpu.get_barrier_semaphore()
    for k in range(1, NT):
        pl.semaphore_signal(barrier, inc=1, device_id=(d, (t + k) % NT), device_id_type=MESH)

    def greet(k, carry):
        pl.semaphore_signal(barrier, inc=1, device_id=((d + k) % NDP, t), device_id_type=MESH)
        return carry

    lax.fori_loop(1, NDP, greet, 0)
    pl.semaphore_wait(barrier, NT - 1 + NDP - 1)

    z_rows = pl.ds(pl.multiple_of(z * Z_ROWS, 16), Z_ROWS)
    x_rows = pl.ds(pl.multiple_of(NZ * Z_ROWS + x * X_ROWS, 16), X_ROWS)

    def slices(j):
        return [
            send(kv_hbm.at[(y + j) % NY, rows], wt.at[NY - j, rows], at_y(j))
            for rows in (z_rows, x_rows)
        ]

    arrives = {2: slices(2), 1: slices(3), 3: slices(1)}

    l_dec.wait()
    l_gain.wait()
    gain = gain_ref[...].reshape(1, D)
    decode = dec_raw[...].astype(F32).reshape(DR, D)
    dg[t] = (decode * gain).astype(BF16)
    A, B = pl.ds(0, DHALF), pl.ds(DHALF, DHALF)

    def block(k, rows, dev):
        return send(dg.at[k, rows], dg.at[k, rows], dev)

    up_a = block(t, A, up)
    dn_b = block(t, B, dn)
    up_b = block(t, B, up)
    dn_a = block(t, A, dn)
    g_core = send(dg.at[t], dg.at[t], core)

    l_q = local_copy(q_hbm, qw, 3)
    l_kv = local_copy(kv_hbm, kvw, 2)
    l_wt = local_copy(kv_hbm.at[y], wt.at[0], 4)
    l_wo = []
    for b in range(NY):
        cols = pl.ds(pl.multiple_of((2 * b + c) * D, 128), D)
        l_wo.append(local_copy(wo_hbm.at[:, cols], wob.at[0, b], 5 + b))

    l_owner.wait()
    l_local.wait()
    mine = (owner_ref[...] * PROMPTS + local_ref[...]).astype(F32)
    ids[d] = jnp.concatenate([mine, jnp.full((1, 64), -1.0, F32)], axis=1)
    send_many(ids, ids, IDS, False)

    ones = jnp.ones((8, D), BF16)

    def squares(value):
        sq = value * value
        high = sq.astype(BF16)
        low = (sq - high.astype(F32)).astype(BF16)
        return nt(ones, high) + nt(ones, low)

    row8 = iota((8, 128), 0)
    parts = [jnp.zeros((8, 128), F32)]

    def prompt_block(i):
        value = prm_raw[i * 128 : (i + 1) * 128].astype(F32)
        ps[c, i * 128 : (i + 1) * 128] = (value * gain).astype(BF16)
        parts[0] = jnp.where(row8 == i, squares(value), parts[0])

    def same(ref, dev):
        return send(ref, ref, dev)

    def spread_slices(slot):
        for copy in arrives[slot]:
            copy.wait_recv()
        copies = [same(wt.at[slot, x_rows], at_x(k)) for k in (2, 1, 3)]
        copies += [same(wt.at[slot, z_rows], at_z(k)) for k in (4, 3, 5, 2, 6, 1, 7)]
        return copies

    l_prm.wait()
    for i in range(4):
        prompt_block(i)
    spread = {2: spread_slices(2)}
    for i in range(4, PR // 128):
        prompt_block(i)
    ps_copy = same(ps.at[c], core)
    sg[t, 0:8] = parts[0]
    part = jnp.zeros((8, 128), F32)
    for i in range(DR // 128):
        part = jnp.where(row8 == i, squares(decode[i * 128 : (i + 1) * 128]), part)
    sg[t, 8:16] = part
    sq = [same(sg.at[t], (d, (t + k) % NT)) for k in range(1, NT)]

    spread[1] = spread_slices(1)
    spread[3] = spread_slices(3)

    r256, c256 = iota((DR, DR), 0), iota((DR, DR), 1)
    owners = jnp.broadcast_to(owner_ref[...].astype(F32), (8, 64)).astype(BF16)
    expand = jnp.where(iota((64, DR), 0) == (iota((64, DR), 1) >> 2), 1.0, 0.0).astype(BF16)
    owner_row = nn(owners, expand)[0:1].astype(jnp.int32)
    expand = jnp.where((iota((DR, 64), 0) >> 2) == iota((DR, 64), 1), 1.0, 0.0).astype(BF16)
    owner_col = nt(expand, owners)[:, 0:1].astype(jnp.int32)
    alike = (owner_col == owner_row) & ((r256 & 3) == (c256 & 3))
    rank_row = jnp.sum(jnp.where(alike & (r256 < c256), 1, 0), axis=0, keepdims=True)
    rank_col = jnp.sum(jnp.where(alike & (c256 < r256), 1, 0), axis=1, keepdims=True)
    lane_row = iota((1, DR), 1)
    lane_col = iota((DR, 1), 0)
    target_row = owner_row * SLOTS + rank_row * 4 + (lane_row & 3)
    target_col = owner_col * SLOTS + rank_col * 4 + (lane_col & 3)
    n_slots = NDP * SLOTS

    below, above, opposite = block_of(NY - 1), block_of(1), block_of(2)
    up_a.wait_recv()
    up_fa = block(below, A, up)
    dn_b.wait_recv()
    dn_fb = block(above, B, dn)
    relays = [block(below, A, core), block(above, B, core)]
    up_b.wait_recv()
    relays.append(block(below, B, core))
    dn_a.wait_recv()
    relays.append(block(above, A, core))

    l_q.wait()
    l_kv.wait()

    def project(k, first=False):
        add_q = nn(dg[k], qw[k])
        add_kv = nn(dg[k], kvw[k // 2, pl.ds(pl.multiple_of(k % 2 * D, D), D)])
        if first:
            acc[:, : GROUP * HEAD] = add_q
            acc[:, GROUP * HEAD :] = add_kv
        else:
            acc[:, : GROUP * HEAD] += add_q
            acc[:, GROUP * HEAD :] += add_kv

    project(t, True)

    ps_copy.wait_recv()
    l_wt.wait()

    def partial(j, row, rows):
        return nn(ps[0, row : row + rows], wt[j, :D]) + nn(ps[1, row : row + rows], wt[j, D:])

    def rp(n, dev):
        return send(rp_send.at[n], rp_recv.at[n], dev)

    def slot_ready(slot):
        for copy in spread[slot]:
            copy.wait_recv()

    slot_ready(2)
    rp_send[0] = partial(2, 0, HALF).astype(BF16)
    rp0 = rp(0, dn)
    rp_send[1] = partial(2, HALF, HALF).astype(BF16)
    rp1 = rp(1, up)
    project(below)
    project(above)

    up_fa.wait_recv()
    relays.append(block(opposite, A, core))
    dn_fb.wait_recv()
    relays.append(block(opposite, B, core))

    slot_ready(1)
    rp_send[2] = partial(1, 0, HALF).astype(BF16)
    rp2 = rp(2, up)
    slot_ready(3)
    rp_send[3] = partial(3, HALF, HALF).astype(BF16)
    rp3 = rp(3, dn)

    project(opposite)
    g_core.wait_recv()
    project(block_of(0) + oc - c)
    for copy in relays:
        copy.wait_recv()
    for j in range(1, NY):
        project(block_of(j) + oc - c)

    for copy in sq:
        copy.wait_recv()
    total = sg[0]
    for k in range(1, NT):
        total = total + sg[k]
    factor = lax.rsqrt(total / MODEL_WIDTH + EPSILON)
    for i in range((PR + DR) // 128):
        rcol[i * 128 : (i + 1) * 128] = jnp.broadcast_to(factor[i : i + 1], (128, 128)).T

    scale = rcol[PR : PR + DR]
    for i in range(WIDTH // 128):
        pj[:, i * 128 : (i + 1) * 128] = (acc[:, i * 128 : (i + 1) * 128] * scale).astype(BF16)
    for i in range(4):
        rows = iota((n_slots // 4, DR), 0) + i * (n_slots // 4)
        pick = jnp.where(rows == target_row, 1.0, 0.0).astype(BF16)
        placed = nn(pick, pj[:, : GROUP * HEAD]).astype(BF16)
        qo[i * 8 : (i + 1) * 8] = placed.reshape(8, SLOTS, GROUP * HEAD)
    qr[d] = qo[d]
    send_many(qo, qr, QX, True)

    part = partial(3, 0, HALF)
    rp0.wait_recv()
    rp_send[4] = (part + rp_recv[0].astype(F32)).astype(BF16)
    rp4 = rp(4, dn)
    part = partial(1, HALF, HALF)
    rp1.wait_recv()
    rp_send[5] = (part + rp_recv[1].astype(F32)).astype(BF16)
    rp5 = rp(5, up)
    own_sum[:HALF] = partial(0, 0, HALF)
    own_sum[HALF:] = partial(0, HALF, HALF)

    wo_copies = []
    for b in range(NY):
        cols = pl.ds(pl.multiple_of((2 * b + oc) * D, 128), D)
        wo_copies.append(send(wo_hbm.at[:, cols], wob.at[1, b], core))

    root = float(HEAD) ** -0.5
    rows3 = GROUP * 128

    def heads_down(value):
        return jnp.concatenate([value[:, h * HEAD : (h + 1) * HEAD] for h in range(GROUP)], axis=0)

    def heads_across(value):
        return jnp.concatenate([value[h * 128 : (h + 1) * 128] for h in range(GROUP)], axis=1)

    for i in range(2):
        rows = pj[i * 128 : (i + 1) * 128]
        r, cc = iota((rows3, 128), 0) & 127, iota((rows3, 128), 1)
        usable = ((r >> 2) == (cc >> 2)) & ((cc & 3) <= (r & 3))
        query = heads_down(rows)
        own = nt(query, rows[:, GROUP * HEAD : GROUP * HEAD + HEAD]) * root
        own = jnp.where(usable, own, HUGE_NEGATIVE)
        own_top = jnp.max(own, axis=1, keepdims=True)
        own_weights = jnp.where(usable, jnp.exp(own - own_top), 0.0)
        own_mass = jnp.sum(own_weights, axis=1, keepdims=True)
        mine_ref[i, 0] = nn(own_weights.astype(BF16), rows[:, GROUP * HEAD + HEAD :])
        mine_ref[i, 1] = jnp.broadcast_to(own_top, (rows3, 128))
        mine_ref[i, 2] = jnp.broadcast_to(own_mass, (rows3, 128))

    l_lengths.wait()
    wait_many(ids, IDS)
    which = jnp.concatenate([ids[s] for s in range(NDP)], axis=0)
    local = which - (PROMPTS * d).astype(F32)
    match = (local >= 0.0) & (local < float(PROMPTS))
    before = jnp.where(iota((128, 128), 0) < iota((128, 128), 1), 1.0, 0.0).astype(BF16)
    rank = nn(jnp.where(match, 1.0, 0.0).astype(BF16), before)
    lane = iota((NDP, 128), 1)
    table = jnp.zeros((NDP, 128), F32)
    for k in range(4):
        at_k = jnp.sum(
            jnp.where(match & (rank == float(k)), local, 0.0), axis=1, keepdims=True
        )
        table = jnp.where(lane == k, at_k, table)
    table = table.astype(BF16)
    for i in range(4):
        sub = iota((128, NDP), 0)
        spread = jnp.where((sub >> 4) + 8 * i == iota((128, NDP), 1), 1.0, 0.0).astype(BF16)
        wide = nn(spread, table)
        mine = iota((128, 128), 1) == ((iota((128, 128), 0) >> 2) & 3)
        pid = jnp.sum(jnp.where(mine, wide, 0.0), axis=1, keepdims=True)
        pid_ref[i * 128 : (i + 1) * 128] = jnp.broadcast_to(pid, (128, 128))
        lens = jnp.zeros((128, 1), F32)
        for p in range(PROMPTS):
            lens = jnp.where(pid == float(p), lengths_ref[PROMPTS * d + p].astype(F32), lens)
        len_ref[i * 128 : (i + 1) * 128] = jnp.broadcast_to(lens, (128, 128))

    rp2.wait_recv()
    rp4.wait_recv()

    def finish_rows(base, one_slot, two_slot):
        def one(i, carry):
            at = pl.ds(pl.multiple_of(i * 128, 128), 128)
            there = pl.ds(pl.multiple_of(base + i * 128, 128), 128)
            value = own_sum[there] + rp_recv[one_slot, at].astype(F32) + rp_recv[two_slot, at].astype(F32)
            factor = rcol[there]
            kt[base // 128 + i] = (value[:, :HEAD] * factor).T.astype(BF16)
            vc[there] = (value[:, HEAD:] * factor).astype(BF16)
            return carry

        lax.fori_loop(0, HALF // 128, one, 0)

    finish_rows(0, 2, 4)
    rp3.wait_recv()
    rp5.wait_recv()
    finish_rows(HALF, 3, 5)

    wait_many(qr, QX)
    def thrice(value):
        return jnp.concatenate([value] * GROUP, axis=0)

    def attend(step, carry):
        i = (z // 2 + step) % 4
        at = pl.ds(pl.multiple_of(i * 128, 128), 128)
        sources = pl.ds(pl.multiple_of(i * 8, 8), 8)
        query = heads_down(qr[sources].reshape(128, GROUP * HEAD))
        pid = thrice(pid_ref[at, 0:1])
        lens = thrice(len_ref[at, 0:1])
        live = iota((rows3, LP), 1).astype(F32) < lens
        scores = None
        for p in range(PROMPTS):
            keys = jnp.concatenate([kt[2 * p], kt[2 * p + 1]], axis=1)
            found = nn(query, keys)
            scores = found if p == 0 else jnp.where(pid == float(p), found, scores)
        scores = jnp.where(live, scores * root, HUGE_NEGATIVE)
        top = jnp.max(scores, axis=1, keepdims=True)
        weights = jnp.where(live, jnp.exp(scores - top), 0.0)
        mass = jnp.sum(weights, axis=1, keepdims=True)
        blended = jnp.zeros((rows3, HEAD), F32)
        for p in range(PROMPTS):
            masked = jnp.where(pid == float(p), weights, 0.0).astype(BF16)
            blended = blended + nn(masked, vc[p * LP : (p + 1) * LP])
        result = heads_across((blended / mass).astype(BF16))
        ro_[sources] = result.reshape(8, SLOTS, GROUP * HEAD)
        level = top + jnp.log(mass)
        row, lane = iota((128, 128), 0), iota((128, 128), 1)
        wide = jnp.zeros((128, 128), F32)
        for h in range(GROUP):
            wide = jnp.where((lane >> 4) == h, level[h * 128 : (h + 1) * 128], wide)
        wide = jnp.where((lane & 15) == (row & 15), wide, 0.0)
        gather = jnp.where((iota((8, 128), 1) >> 4) == iota((8, 128), 0), 1.0, 0.0)
        levels = exact(gather, wide)
        for k in range(8):
            lo[i * 8 + k] = levels[k : k + 1]

        def give(k, carry):
            to = i * 8 + k

            @pl.when(to != d)
            def _():
                remote(ro_.at[to], rr.at[d], RX, (to, t)).start()
                remote(lo.at[to], lr.at[d], LX, (to, t)).start()

            return carry

        lax.fori_loop(0, 8, give, 0)
        return carry

    lax.fori_loop(0, 4, attend, 0)
    rr[d] = ro_[d]
    lr[d] = lo[d]
    wait_many(lr, LX)
    wait_many(rr, RX)

    levels = jnp.concatenate([lr[s] for s in range(NDP)], axis=0)
    prefix = rr[...].reshape(n_slots, GROUP * HEAD)
    for i in range(2):
        target = target_col[i * 128 : (i + 1) * 128]
        take = jnp.where(iota((128, n_slots), 1) == target, 1.0, 0.0).astype(BF16)
        found = heads_down(nn(take, prefix))
        owner = jnp.where(iota((128, NDP), 1) == (target >> 4), 1.0, 0.0)
        level = exact(owner, levels)
        lane = iota((128, 128), 1)
        level = jnp.concatenate(
            [
                jnp.sum(jnp.where(lane == h * 16 + (target & 15), level, 0.0), axis=1, keepdims=True)
                for h in range(GROUP)
            ],
            axis=0,
        )
        own_blended, own_top, own_mass = mine_ref[i, 0], mine_ref[i, 1], mine_ref[i, 2]
        highest = jnp.maximum(level, own_top)
        one, two = jnp.exp(level - highest), jnp.exp(own_top - highest)
        merged = (found * one + own_blended * two) / (one + own_mass * two)
        ax[c, i * 128 : (i + 1) * 128] = heads_across(merged.astype(BF16))
    ax_copy = same(ax.at[c], core)
    for copy in l_wo:
        copy.wait()
    for copy in wo_copies:
        copy.wait_recv()
    ax_copy.wait_recv()

    def out_partial(j, row):
        b = (y + j) % NY
        at = pl.ds(row, DHALF)
        return nn(ax[c, at], wob[0, b]) + nn(ax[oc, at], wob[1, b])

    def out_send(n, j, row, extra, dev):
        value = out_partial(j, row)
        if extra is not None:
            value = value + rs_recv[extra].astype(F32)
        rs_send[n] = value.astype(BF16)
        return send(rs_send.at[n], rs_recv.at[n], dev)

    o0 = out_send(0, 2, 0, None, dn)
    o1 = out_send(1, 2, DHALF, None, up)
    o2 = out_send(2, 1, 0, None, up)
    o3 = out_send(3, 3, DHALF, None, dn)
    o0.wait_recv()
    o4 = out_send(4, 3, 0, 0, dn)
    o1.wait_recv()
    o5 = out_send(5, 1, DHALF, 1, up)
    own_a = out_partial(0, 0)
    o2.wait_recv()
    o4.wait_recv()
    own_a = own_a + rs_recv[2].astype(F32) + rs_recv[4].astype(F32)
    out_ref[: DHALF // 4] = own_a.reshape(DHALF // 4, 4, D).astype(BF16)
    first, second = pl.ds(0, DHALF // 4), pl.ds(DHALF // 4, DHALF // 4)
    out_a = local_copy(out_ref.at[first], out_hbm.at[first], 13)
    own_b = out_partial(0, DHALF)
    o3.wait_recv()
    o5.wait_recv()
    own_b = own_b + rs_recv[3].astype(F32) + rs_recv[5].astype(F32)
    out_ref[DHALF // 4 :] = own_b.reshape(DHALF // 4, 4, D).astype(BF16)
    out_b = local_copy(out_ref.at[second], out_hbm.at[second], 14)

    out_a.wait()
    out_b.wait()
    for copy in sent:
        copy.wait_send()
    for ref, n in ((ids, IDS), (qo, QX), (ro_, RX), (lo, LX)):
        many(ref, ss.at[n]).wait()


def shards(
    prompt_states, prompt_lengths, decode_states, sample_owner, sample_local,
    norm_gain, kv_weight, q_weight, output_weight,
):
    hbm = pl.BlockSpec(memory_space=pl.ANY)
    out = pl.pallas_call(
        kernel,
        out_shape=jax.ShapeDtypeStruct((DR // 4, 4, D), BF16),
        in_specs=[hbm] * 9,
        out_specs=hbm,
        scratch_shapes=[
            pltpu.VMEM((D,), F32),
            pltpu.VMEM((1, 64), jnp.int32),
            pltpu.VMEM((1, 64), jnp.int32),
            pltpu.SMEM((NDP * PROMPTS,), jnp.int32),
            pltpu.VMEM((DR // 4, 4, D), BF16),
            pltpu.VMEM((DR // 4, 4, D), BF16),
            pltpu.VMEM((PR, D), BF16),
            pltpu.VMEM((NT, DR, D), BF16),
            pltpu.VMEM((NC, PR, D), BF16),
            pltpu.VMEM((NT, 16, 128), F32),
            pltpu.VMEM((NDP, 1, 128), F32),
            pltpu.VMEM((NT, D, GROUP * HEAD), BF16),
            pltpu.VMEM((NY, 2 * D, 2 * HEAD), BF16),
            pltpu.VMEM((NY, 2 * D, 2 * HEAD), BF16),
            pltpu.VMEM((NC, NY, GROUP * HEAD, D), BF16),
            pltpu.VMEM((6, HALF, 2 * HEAD), BF16),
            pltpu.VMEM((6, HALF, 2 * HEAD), BF16),
            pltpu.VMEM((PR, 2 * HEAD), F32),
            pltpu.VMEM((PR // 128, HEAD, 128), BF16),
            pltpu.VMEM((PR, HEAD), BF16),
            pltpu.VMEM((DR, WIDTH), F32),
            pltpu.VMEM((DR, WIDTH), BF16),
            pltpu.VMEM((NDP, SLOTS, GROUP * HEAD), BF16),
            pltpu.VMEM((NDP, SLOTS, GROUP * HEAD), BF16),
            pltpu.VMEM((NDP, 1, 128), F32),
            pltpu.VMEM((NDP, 1, 128), F32),
            pltpu.VMEM((2, 3, GROUP * 128, 128), F32),
            pltpu.VMEM((NDP, SLOTS, GROUP * HEAD), BF16),
            pltpu.VMEM((NDP, SLOTS, GROUP * HEAD), BF16),
            pltpu.VMEM((NC, DR, GROUP * HEAD), BF16),
            pltpu.VMEM((6, DHALF, D), BF16),
            pltpu.VMEM((6, DHALF, D), BF16),
            pltpu.VMEM((NDP * SLOTS, 128), F32),
            pltpu.VMEM((NDP * SLOTS, 128), F32),
            pltpu.VMEM((PR + DR, 128), F32),
            pltpu.SemaphoreType.DMA((N_SEM,)),
            pltpu.SemaphoreType.DMA((N_SEM,)),
            pltpu.SemaphoreType.DMA((15,)),
        ],
        compiler_params=pltpu.CompilerParams(
            collective_id=0, has_side_effects=True, vmem_limit_bytes=56 * 1024 * 1024
        ),
    )(
        decode_states,
        prompt_states.reshape(PR, D),
        norm_gain,
        sample_owner.reshape(1, 64),
        sample_local.reshape(1, 64),
        prompt_lengths,
        kv_weight.reshape(NY, 2 * D, 2 * HEAD),
        q_weight.reshape(NT, D, GROUP * HEAD),
        output_weight.reshape(GROUP * HEAD, MODEL_WIDTH),
    )
    return out


def solution(mesh):
    placed = (
        P("dp", None, "tensor"),
        P(),
        P("dp", None, "tensor"),
        P("dp", None),
        P("dp"),
        P("tensor"),
        P(None, "tensor", None),
        P(None, "tensor", None),
        P("tensor", None, None),
    )
    return jax.shard_map(
        shards, mesh=mesh, in_specs=placed, out_specs=P("dp", None, "tensor"), check_vma=False
    )
```

time: 90.1 us -> 82.5 us (0.916)
  Pallas kernels: 88.1 us -> 80.3 us
    pallas_call x1, Pallas kernels: 88.1 us -> 80.3 us  [shards(): pl.pallas_call(kernel, out_shape=jax.ShapeDtypeStruct((DR // 4, 4, D), BF...]
where the time goes in v3:
time: 82.5 us; the launch traced here: 82.1 us
  Pallas kernels  80.3 us (97%)
  local copies, waits for them, and re-layouts  1.81 us (2%)
    pallas_call x1, Pallas kernels, shards(): pl.pallas_call(kernel, out_shape=jax.ShapeDtypeStruct((DR // 4, 4, D), BF...  80.3 us
    unnamed x1, local copies, waits for them, and re-layouts  1.81 us

profile of v3, /device:TPU:1, one launch (start us, length us, event | category | flops | bytes accessed | tf_op | source)
XLA Modules:
  0.0 82.1 jit_solution(15346318666292862577)
XLA Ops:
  0.0 80.3 %shard_map.91 = bf16[64,4,640]{2,1,0:T(4,128)(2,1)} custom-call(bf16[64,4,640]{2,1,0:T(4,128)(2,1)} %decode_hbm.1, bf16[1024,640]{1,0:T(8,128)(2,1)} %bitcast.9, f32[640]{0:T(1024)} %gain_hbm.1, s32[1,64]{1,0:T(1,128)} %bitcast.10, s32[1,64]{1,0:T(1,128)} %bitcast.11, s32[128]{0:T(128)} %lengths_hbm.1, bf16[4,1280,256]{2,1,0:T(8,128)(2,1)} %bitcast.8, ...), custom_call_target="tpu_custom_call" | custom-call | tf_op jit(solution)/shard_map/pallas_call | solution.py:541
  80.3 1.8 %copy.11 = bf16[64,4,640]{2,1,0:T(4,128)(2,1)} copy(bf16[64,4,640]{2,1,0:T(4,128)(2,1)} %shard_map.91) | data formatting | bytes 655360

commit v4 on v3

--- a/solution.py
+++ b/solution.py
@@ -57,7 +57,7 @@
     kv_hbm, q_hbm, wo_hbm,
     out_hbm,
     gain_ref, owner_ref, local_ref, lengths_ref, out_ref, dec_raw, prm_raw, dg, ps, sg, ids, qw, kvw, wt, wob,
-    rp_send, rp_recv, own_sum, kt, vc, acc, pj, qo, qr, lo, lr, mine_ref, ro_, rr, ax, rs_send, rs_recv,
+    rp_send, rp_recv, own_sum, kt, vc, acc, pj, qo, qr, lo, lr, mine_ref, take_ref, ro_, rr, ax, rs_send, rs_recv,
     pid_ref, len_ref, rcol,
     ss, rs, ls,
 ):
@@ -106,12 +106,16 @@
         return pltpu.make_async_copy(part, part, sem)
 
     def send_many(ref, to_ref, n, per_target):
-        def one(k, carry):
-            to = (d + k) % NDP
+        def to_one(to):
             remote(ref.at[to if per_target else d], to_ref.at[d], n, (to, t)).start()
+
+        def two(k, carry):
+            to_one((d + NDP // 2 - k) % NDP)
+            to_one((d + NDP // 2 + k) % NDP)
             return carry
 
-        lax.fori_loop(1, NDP, one, 0)
+        to_one((d + NDP // 2) % NDP)
+        lax.fori_loop(1, NDP // 2, two, 0)
 
     def wait_many(to_ref, n):
         many(to_ref, rs.at[n]).wait()
@@ -395,7 +399,7 @@
             there = pl.ds(pl.multiple_of(base + i * 128, 128), 128)
             value = own_sum[there] + rp_recv[one_slot, at].astype(F32) + rp_recv[two_slot, at].astype(F32)
             factor = rcol[there]
-            kt[base // 128 + i] = (value[:, :HEAD] * factor).T.astype(BF16)
+            kt[base // 128 + i] = (value[:, :HEAD] * factor).astype(BF16).T
             vc[there] = (value[:, HEAD:] * factor).astype(BF16)
             return carry
 
@@ -411,12 +415,18 @@
         return jnp.concatenate([value] * GROUP, axis=0)
 
     def attend(step, carry):
-        i = (z // 2 + step) % 4
-        at = pl.ds(pl.multiple_of(i * 128, 128), 128)
-        sources = pl.ds(pl.multiple_of(i * 8, 8), 8)
-        query = heads_down(qr[sources].reshape(128, GROUP * HEAD))
-        pid = thrice(pid_ref[at, 0:1])
-        lens = thrice(len_ref[at, 0:1])
+        away = 4 - step
+        planes = [(z + away) % NZ, (z + NZ - away - 4 * (away // 4)) % NZ]
+        four = [pl.ds(pl.multiple_of(plane * NX, NX), NX) for plane in planes]
+        at = [pl.ds(pl.multiple_of(plane * 64, 64), 64) for plane in planes]
+
+        def both(ref):
+            return jnp.concatenate([ref[rows, 0:1] for rows in at], axis=0)
+
+        query = jnp.concatenate([qr[s].reshape(64, GROUP * HEAD) for s in four], axis=0)
+        query = heads_down(query)
+        pid = thrice(both(pid_ref))
+        lens = thrice(both(len_ref))
         live = iota((rows3, LP), 1).astype(F32) < lens
         scores = None
         for p in range(PROMPTS):
@@ -432,7 +442,8 @@
             masked = jnp.where(pid == float(p), weights, 0.0).astype(BF16)
             blended = blended + nn(masked, vc[p * LP : (p + 1) * LP])
         result = heads_across((blended / mass).astype(BF16))
-        ro_[sources] = result.reshape(8, SLOTS, GROUP * HEAD)
+        for n in range(2):
+            ro_[four[n]] = result[n * 64 : (n + 1) * 64].reshape(NX, SLOTS, GROUP * HEAD)
         level = top + jnp.log(mass)
         row, lane = iota((128, 128), 0), iota((128, 128), 1)
         wide = jnp.zeros((128, 128), F32)
@@ -442,10 +453,10 @@
         gather = jnp.where((iota((8, 128), 1) >> 4) == iota((8, 128), 0), 1.0, 0.0)
         levels = exact(gather, wide)
         for k in range(8):
-            lo[i * 8 + k] = levels[k : k + 1]
+            lo[planes[k // 4] * NX + k % 4] = levels[k : k + 1]
 
         def give(k, carry):
-            to = i * 8 + k
+            to = ((z + away) * (1 - k % 2) + (z + NZ - away - 4 * (away // 4)) * (k % 2)) % NZ * NX + k // 2
 
             @pl.when(to != d)
             def _():
@@ -460,15 +471,23 @@
     lax.fori_loop(0, 4, attend, 0)
     rr[d] = ro_[d]
     lr[d] = lo[d]
+    for i in range(2):
+        rows = pl.ds(i * 128, 128)
+        target = target_col[i * 128 : (i + 1) * 128]
+        take_ref[rows] = jnp.where(iota((128, n_slots), 1) == target, 1.0, 0.0).astype(BF16)
     wait_many(lr, LX)
     wait_many(rr, RX)
 
+    for copy in l_wo:
+        copy.wait()
+    for copy in wo_copies:
+        copy.wait_recv()
     levels = jnp.concatenate([lr[s] for s in range(NDP)], axis=0)
+    ax_copies = []
     prefix = rr[...].reshape(n_slots, GROUP * HEAD)
     for i in range(2):
         target = target_col[i * 128 : (i + 1) * 128]
-        take = jnp.where(iota((128, n_slots), 1) == target, 1.0, 0.0).astype(BF16)
-        found = heads_down(nn(take, prefix))
+        found = heads_down(nn(take_ref[i * 128 : (i + 1) * 128], prefix))
         owner = jnp.where(iota((128, NDP), 1) == (target >> 4), 1.0, 0.0)
         level = exact(owner, levels)
         lane = iota((128, 128), 1)
@@ -484,12 +503,7 @@
         one, two = jnp.exp(level - highest), jnp.exp(own_top - highest)
         merged = (found * one + own_blended * two) / (one + own_mass * two)
         ax[c, i * 128 : (i + 1) * 128] = heads_across(merged.astype(BF16))
-    ax_copy = same(ax.at[c], core)
-    for copy in l_wo:
-        copy.wait()
-    for copy in wo_copies:
-        copy.wait_recv()
-    ax_copy.wait_recv()
+        ax_copies.append(same(ax.at[c, pl.ds(i * 128, 128)], core))
 
     def out_partial(j, row):
         b = (y + j) % NY
@@ -503,7 +517,9 @@
         rs_send[n] = value.astype(BF16)
         return send(rs_send.at[n], rs_recv.at[n], dev)
 
+    ax_copies[0].wait_recv()
     o0 = out_send(0, 2, 0, None, dn)
+    ax_copies[1].wait_recv()
     o1 = out_send(1, 2, DHALF, None, up)
     o2 = out_send(2, 1, 0, None, up)
     o3 = out_send(3, 3, DHALF, None, dn)
@@ -571,6 +587,7 @@
             pltpu.VMEM((NDP, 1, 128), F32),
             pltpu.VMEM((NDP, 1, 128), F32),
             pltpu.VMEM((2, 3, GROUP * 128, 128), F32),
+            pltpu.VMEM((DR, NDP * SLOTS), BF16),
             pltpu.VMEM((NDP, SLOTS, GROUP * HEAD), BF16),
             pltpu.VMEM((NDP, SLOTS, GROUP * HEAD), BF16),
             pltpu.VMEM((NC, DR, GROUP * HEAD), BF16),

time: 82.5 us -> 81.2 us (0.984)
  Pallas kernels: 80.3 us -> 79.2 us
    pallas_call x1, Pallas kernels: 80.3 us -> 79.2 us  [shards(): pl.pallas_call(kernel, out_shape=jax.ShapeDtypeStruct((DR // 4, 4, D), BF...]
where the time goes in v4:
time: 81.2 us; the launch traced here: 81.1 us
  Pallas kernels  79.2 us (98%)
  local copies, waits for them, and re-layouts  1.81 us (2%)
    pallas_call x1, Pallas kernels, shards(): pl.pallas_call(kernel, out_shape=jax.ShapeDtypeStruct((DR // 4, 4, D), BF...  79.2 us
    unnamed x1, local copies, waits for them, and re-layouts  1.81 us

profile of v4, /device:TPU:1, one launch (start us, length us, event | category | flops | bytes accessed | tf_op | source)
XLA Modules:
  0.0 81.1 jit_solution(10785540036420584071)
XLA Ops:
  0.0 79.2 %shard_map.91 = bf16[64,4,640]{2,1,0:T(4,128)(2,1)} custom-call(bf16[64,4,640]{2,1,0:T(4,128)(2,1)} %decode_hbm.1, bf16[1024,640]{1,0:T(8,128)(2,1)} %bitcast.9, f32[640]{0:T(1024)} %gain_hbm.1, s32[1,64]{1,0:T(1,128)} %bitcast.10, s32[1,64]{1,0:T(1,128)} %bitcast.11, s32[128]{0:T(128)} %lengths_hbm.1, bf16[4,1280,256]{2,1,0:T(8,128)(2,1)} %bitcast.8, ...), custom_call_target="tpu_custom_call" | custom-call | tf_op jit(solution)/shard_map/pallas_call | solution.py:557
  79.2 1.8 %copy.11 = bf16[64,4,640]{2,1,0:T(4,128)(2,1)} copy(bf16[64,4,640]{2,1,0:T(4,128)(2,1)} %shard_map.91) | data formatting | bytes 655360

commit v5 on v4

--- a/solution.py
+++ b/solution.py
@@ -475,19 +475,14 @@
         rows = pl.ds(i * 128, 128)
         target = target_col[i * 128 : (i + 1) * 128]
         take_ref[rows] = jnp.where(iota((128, n_slots), 1) == target, 1.0, 0.0).astype(BF16)
-    wait_many(lr, LX)
-    wait_many(rr, RX)
-
     for copy in l_wo:
         copy.wait()
     for copy in wo_copies:
         copy.wait_recv()
+    wait_many(lr, LX)
     levels = jnp.concatenate([lr[s] for s in range(NDP)], axis=0)
-    ax_copies = []
-    prefix = rr[...].reshape(n_slots, GROUP * HEAD)
     for i in range(2):
         target = target_col[i * 128 : (i + 1) * 128]
-        found = heads_down(nn(take_ref[i * 128 : (i + 1) * 128], prefix))
         owner = jnp.where(iota((128, NDP), 1) == (target >> 4), 1.0, 0.0)
         level = exact(owner, levels)
         lane = iota((128, 128), 1)
@@ -501,7 +496,16 @@
         own_blended, own_top, own_mass = mine_ref[i, 0], mine_ref[i, 1], mine_ref[i, 2]
         highest = jnp.maximum(level, own_top)
         one, two = jnp.exp(level - highest), jnp.exp(own_top - highest)
-        merged = (found * one + own_blended * two) / (one + own_mass * two)
+        whole = one + own_mass * two
+        mine_ref[i, 0] = own_blended * (two / whole)
+        mine_ref[i, 1] = one / whole
+
+    wait_many(rr, RX)
+    prefix = rr[...].reshape(n_slots, GROUP * HEAD)
+    ax_copies = []
+    for i in range(2):
+        found = heads_down(nn(take_ref[i * 128 : (i + 1) * 128], prefix))
+        merged = found * mine_ref[i, 1] + mine_ref[i, 0]
         ax[c, i * 128 : (i + 1) * 128] = heads_across(merged.astype(BF16))
         ax_copies.append(same(ax.at[c, pl.ds(i * 128, 128)], core))
 

time: 81.2 us -> 81.5 us (level)
  no operation moved by 1% of the time
where the time goes in v5:
time: 81.5 us; the launch traced here: 81.4 us
  Pallas kernels  79.6 us (98%)
  local copies, waits for them, and re-layouts  1.81 us (2%)
    pallas_call x1, Pallas kernels, shards(): pl.pallas_call(kernel, out_shape=jax.ShapeDtypeStruct((DR // 4, 4, D), BF...  79.6 us
    unnamed x1, local copies, waits for them, and re-layouts  1.81 us

profile of v5, /device:TPU:1, one launch (start us, length us, event | category | flops | bytes accessed | tf_op | source)
XLA Modules:
  0.0 81.4 jit_solution(7350532150352300960)
XLA Ops:
  0.0 79.6 %shard_map.91 = bf16[64,4,640]{2,1,0:T(4,128)(2,1)} custom-call(bf16[64,4,640]{2,1,0:T(4,128)(2,1)} %decode_hbm.1, bf16[1024,640]{1,0:T(8,128)(2,1)} %bitcast.9, f32[640]{0:T(1024)} %gain_hbm.1, s32[1,64]{1,0:T(1,128)} %bitcast.10, s32[1,64]{1,0:T(1,128)} %bitcast.11, s32[128]{0:T(128)} %lengths_hbm.1, bf16[4,1280,256]{2,1,0:T(8,128)(2,1)} %bitcast.8, ...), custom_call_target="tpu_custom_call" | custom-call | tf_op jit(solution)/shard_map/pallas_call | solution.py:561
  79.6 1.8 %copy.11 = bf16[64,4,640]{2,1,0:T(4,128)(2,1)} copy(bf16[64,4,640]{2,1,0:T(4,128)(2,1)} %shard_map.91) | data formatting | bytes 655360
